TPU v7x, 32 devices: a whole 2x2x4 slice. The times are simulated.
32 devices in a mesh: section: 2 (over x), shard: 4 (over y, core), replica: 4 (over z).
Axes of the slice: x: 2, y: 2, z: 4, core: 2. Of those that a mesh axis runs over, the one named last changes fastest.
Arguments:
- inputs: bfloat16 [4096, 576], P(('shard', 'replica')), may hold values from -6 to 6
- segments: int32 [32, 128], P(('shard', 'replica')), may hold values from 0 to 3, never falling along the last dimension, each value on 1 to 64 neighbouring positions
- cotangent: bfloat16 [4096, 576], P(('shard', 'replica')), may hold values from -6 to 6
- attn_gain: float32 [2, 576], P('section'), may hold values from 0.1 to 1.9
- qkv_weight: bfloat16 [2, 576, 960], P('section', 'shard'), may hold values from -0.25 to 0.25
- out_weight: bfloat16 [2, 576, 576], P('section', 'shard'), may hold values from -0.75 to 0.75
- ffn_gain: float32 [2, 576], P('section'), may hold values from 0.1 to 1.9
- gate_up_weight: bfloat16 [2, 576, 3072], P('section', 'shard'), may hold values from -0.25 to 0.25
- down_weight: bfloat16 [2, 1536, 576], P('section', 'shard'), may hold values from -0.15625 to 0.15625
Outputs:
- activations: bfloat16 [2, 4096, 576], P('section', ('shard', 'replica'))
- input_grads: bfloat16 [2, 4096, 576], P('section', ('shard', 'replica'))
- attn_gain_grad: float32 [2, 576], P('section', 'shard')
- qkv_grad: float32 [2, 576, 960], P('section', 'shard')
- out_grad: float32 [2, 576, 576], P('section', 'shard')
- ffn_gain_grad: float32 [2, 576], P('section', 'shard')
- gate_up_grad: float32 [2, 576, 3072], P('section', 'shard')
- down_grad: float32 [2, 1536, 576], P('section', 'shard')
Inputs may be any that keep to these rules, and one draw needn't show every extreme that they name: `segments`: in each sequence the document numbers never fall; every document has 1 to 64 tokens, and some document exactly 64.
All inputs are finite; a program needn't handle non-finite values.
Results may differ from a plain program's by a relative error of at most 0.02.
Values may be sent and summed in bfloat16 or wider, within the bound.
A program may use at most 128 MiB of HBM per device.

v0:
```python
import math

import jax
import jax.numpy as jnp
from jax import lax
from jax.sharding import PartitionSpec as P

HEADS = 9
KV = 3
HD = 64
FF = 1536


norm_epsilon = 1e-05
rope_base = 100000.0
masked_value = -1e30


def from_behind(block, axis, distance):
    devices = range(lax.axis_size(axis))
    route = [(i - distance, i) for i in devices if i - distance in devices]
    return lax.ppermute(block, axis, route)


def geometry(segment_ids):
    count_cols = segment_ids.shape[-1]
    column = jnp.arange(count_cols, dtype=jnp.int32)
    previous = jnp.concatenate([segment_ids[..., :1], segment_ids[..., :-1]], axis=-1)
    doc_marks = jnp.where(segment_ids != previous, column, 0)
    doc_starts = lax.cummax(doc_marks, axis=doc_marks.ndim - 1)
    positions = (column - doc_starts).astype(jnp.float32)
    allowed = (segment_ids[..., :, None] == segment_ids[..., None, :]) & (
        column[:, None] >= column[None, :]
    )
    half_width = HD // 2
    frequency = jnp.exp(
        -(jnp.arange(half_width, dtype=jnp.float32) * (2.0 / HD)) * math.log(rope_base)
    )
    angles = positions[..., None] * frequency
    return (allowed, jnp.cos(angles), jnp.sin(angles))


def rotate(tensor, cosine_table, sine_table):
    half_width = tensor.shape[-1] // 2
    first_half = tensor[..., :half_width]
    second_half = tensor[..., half_width:]
    cosine_table = cosine_table[..., None, :]
    sine_table = sine_table[..., None, :]
    return jnp.concatenate(
        [
            first_half * cosine_table - second_half * sine_table,
            second_half * cosine_table + first_half * sine_table,
        ],
        axis=-1,
    )


def unrotate(tensor, cosine_table, sine_table):
    half_width = tensor.shape[-1] // 2
    first_half = tensor[..., :half_width]
    second_half = tensor[..., half_width:]
    cosine_table = cosine_table[..., None, :]
    sine_table = sine_table[..., None, :]
    return jnp.concatenate(
        [
            first_half * cosine_table + second_half * sine_table,
            second_half * cosine_table - first_half * sine_table,
        ],
        axis=-1,
    )


def masked_scores(query_rows, key_rows, allowed):
    scores = jnp.einsum(
        "qkrd,tkd->krqt", query_rows, key_rows, preferred_element_type=jnp.float32
    ) * HD ** (-0.5)
    return jnp.where(allowed, scores, masked_value)


def norm_back(residual, stream, inverse, gain_row, grad_out):
    grad_gain = jnp.sum(grad_out * stream * inverse, axis=0)
    grad_hat = grad_out * gain_row
    inner = jnp.mean(grad_hat * stream, axis=-1, keepdims=True)
    return (residual + inverse * (grad_hat - stream * inverse * inverse * inner), grad_gain)


def layer_forward(layer_in, weights, geom):
    gain_attn, qkv_layer, out_layer, gain_ffn, gate_up_layer, down_layer = weights
    allowed, cosine_table, sine_table = geom
    stream = layer_in.astype(jnp.float32)
    length = stream.shape[0]
    inv_attn = lax.rsqrt(jnp.mean(stream * stream, axis=-1, keepdims=True) + norm_epsilon)
    normed = (stream * inv_attn * gain_attn).astype(jnp.bfloat16)
    projected = jnp.dot(normed, qkv_layer, preferred_element_type=jnp.float32)
    query_rows = projected[:, : HEADS * HD].reshape(length, HEADS, HD)
    key_rows = projected[:, HEADS * HD : (HEADS + KV) * HD].reshape(length, KV, HD)
    value_rows = projected[:, (HEADS + KV) * HD :].reshape(length, KV, HD).astype(jnp.bfloat16)
    query_rows = (
        rotate(query_rows, cosine_table, sine_table)
        .astype(jnp.bfloat16)
        .reshape(length, KV, HEADS // KV, HD)
    )
    key_rows = rotate(key_rows, cosine_table, sine_table).astype(jnp.bfloat16)
    scores = masked_scores(query_rows, key_rows, allowed)
    row_max = jnp.max(scores, axis=-1, keepdims=True)
    row_exp = jnp.exp(scores - row_max)
    row_sum = jnp.sum(row_exp, axis=-1, keepdims=True)
    attn_probs = row_exp / row_sum
    log_total = row_max + jnp.log(row_sum)
    attended = jnp.einsum(
        "krqt,tkd->qkrd",
        attn_probs.astype(jnp.bfloat16),
        value_rows,
        preferred_element_type=jnp.float32,
    )
    attended = attended.reshape(length, HEADS * HD).astype(jnp.bfloat16)
    middle = stream + jnp.dot(attended, out_layer, preferred_element_type=jnp.float32)
    inv_ffn = lax.rsqrt(jnp.mean(middle * middle, axis=-1, keepdims=True) + norm_epsilon)
    ffn_normed = (middle * inv_ffn * gain_ffn).astype(jnp.bfloat16)
    gate_up = jnp.dot(ffn_normed, gate_up_layer, preferred_element_type=jnp.float32)
    hidden = (jax.nn.silu(gate_up[:, :FF]) * gate_up[:, FF:]).astype(jnp.bfloat16)
    result = middle + jnp.dot(hidden, down_layer, preferred_element_type=jnp.float32)
    stored = (
        layer_in,
        inv_attn,
        normed,
        query_rows,
        key_rows,
        value_rows,
        log_total,
        attended,
        middle,
        inv_ffn,
        ffn_normed,
        gate_up,
        hidden,
    )
    return (result, stored)


def layer_backward(incoming, weights, geom, stored):
    gain_attn, qkv_layer, out_layer, gain_ffn, gate_up_layer, down_layer = weights
    allowed, cosine_table, sine_table = geom
    (
        layer_in,
        inv_attn,
        normed,
        query_rows,
        key_rows,
        value_rows,
        log_total,
        attended,
        middle,
        inv_ffn,
        ffn_normed,
        gate_up,
        hidden,
    ) = stored
    stream = layer_in.astype(jnp.float32)
    length = stream.shape[0]
    out_rounded = incoming.astype(jnp.bfloat16)
    grad_hidden = jnp.einsum(
        "sd,fd->sf", out_rounded, down_layer, preferred_element_type=jnp.float32
    )
    gate_part = gate_up[:, :FF]
    up_part = gate_up[:, FF:]
    gate_sigmoid = jax.nn.sigmoid(gate_part)
    gate_silu = gate_part * gate_sigmoid
    grad_gate = grad_hidden * up_part * gate_sigmoid * (1.0 + gate_part * (1.0 - gate_sigmoid))
    grad_gu = jnp.concatenate([grad_gate, grad_hidden * gate_silu], axis=-1).astype(jnp.bfloat16)
    grad_fnorm = jnp.einsum("se,de->sd", grad_gu, gate_up_layer, preferred_element_type=jnp.float32)
    grad_middle, grad_gain_ffn = norm_back(incoming, middle, inv_ffn, gain_ffn, grad_fnorm)
    mid_rounded = grad_middle.astype(jnp.bfloat16)
    grad_att = jnp.einsum("sd,cd->sc", mid_rounded, out_layer, preferred_element_type=jnp.float32)
    grad_att = grad_att.astype(jnp.bfloat16).reshape(length, KV, HEADS // KV, HD)
    scores = masked_scores(query_rows, key_rows, allowed)
    attn_probs = jnp.exp(scores - log_total)
    grad_values = jnp.einsum(
        "krqt,qkrd->tkd",
        attn_probs.astype(jnp.bfloat16),
        grad_att,
        preferred_element_type=jnp.float32,
    )
    grad_probs = jnp.einsum(
        "qkrd,tkd->krqt", grad_att, value_rows, preferred_element_type=jnp.float32
    )
    inner = jnp.sum(attn_probs * grad_probs, axis=-1, keepdims=True)
    grad_scores = (attn_probs * (grad_probs - inner)).astype(jnp.bfloat16)
    grad_query = jnp.einsum(
        "krqt,tkd->qkrd", grad_scores, key_rows, preferred_element_type=jnp.float32
    ) * HD ** (-0.5)
    grad_keys = jnp.einsum(
        "krqt,qkrd->tkd", grad_scores, query_rows, preferred_element_type=jnp.float32
    ) * HD ** (-0.5)
    grad_query = unrotate(grad_query.reshape(length, HEADS, HD), cosine_table, sine_table).reshape(
        length, HEADS * HD
    )
    grad_keys = unrotate(grad_keys, cosine_table, sine_table).reshape(length, KV * HD)
    grad_projected = jnp.concatenate(
        [grad_query, grad_keys, grad_values.reshape(length, KV * HD)], axis=-1
    ).astype(jnp.bfloat16)
    grad_normed = jnp.einsum(
        "se,de->sd", grad_projected, qkv_layer, preferred_element_type=jnp.float32
    )
    grad_stream, grad_gain_attn = norm_back(grad_middle, stream, inv_attn, gain_attn, grad_normed)
    operands = (
        normed,
        grad_projected,
        attended,
        mid_rounded,
        ffn_normed,
        grad_gu,
        hidden,
        out_rounded,
    )
    return (grad_stream, (grad_gain_attn, grad_gain_ffn), operands)


def shards(
    inputs,
    segments,
    cotangent,
    attn_gain,
    qkv_weight,
    out_weight,
    ffn_gain,
    gate_up_weight,
    down_weight,
):
    sections = lax.axis_size("section")
    section_index = lax.axis_index("section")
    batches, length = segments.shape
    model_width = inputs.shape[1]
    qkv_full, out_full, gate_up_full, down_full = (
        lax.all_gather(qkv_weight, "shard", axis=1, tiled=True),
        lax.all_gather(out_weight, "shard", axis=1, tiled=True),
        lax.all_gather(gate_up_weight, "shard", axis=1, tiled=True),
        lax.all_gather(down_weight, "shard", axis=1, tiled=True),
    )
    weights = (attn_gain[0], qkv_full[0], out_full[0], ffn_gain[0], gate_up_full[0], down_full[0])
    allowed_all, cosine_all, sine_all = geometry(segments)
    own_rows = inputs.reshape(batches, length, model_width)
    upstream = cotangent.reshape(batches, length, model_width)
    tick_count = batches + sections - 1

    def geometry_of(micro_pick):
        return tuple(
            (
                lax.dynamic_index_in_dim(member, micro_pick, 0, keepdims=False)
                for member in (allowed_all, cosine_all, sine_all)
            )
        )

    outputs_buffer = jnp.zeros((batches, length, model_width), jnp.bfloat16)
    stored_list = []
    outgoing = jnp.zeros((length, model_width), jnp.bfloat16)
    for tick_index in range(tick_count):
        micro_index = tick_index - section_index
        is_valid = (micro_index >= 0) & (micro_index < batches)
        micro_pick = jnp.clip(micro_index, 0, batches - 1)
        if tick_index > 0:
            arrived = from_behind(outgoing, "section", 1)
        else:
            arrived = outgoing
        layer_in = jnp.where(section_index == 0, own_rows[min(tick_index, batches - 1)], arrived)
        result, stored = layer_forward(layer_in, weights, geometry_of(micro_pick))
        outgoing = result.astype(jnp.bfloat16)
        outputs_buffer = jnp.where(
            is_valid,
            lax.dynamic_update_index_in_dim(outputs_buffer, outgoing, micro_pick, 0),
            outputs_buffer,
        )
        stored_list.append(stored)
    stacked = jax.tree.map(lambda *members: jnp.stack(members), *stored_list)
    gain_attn_sum = jnp.zeros((model_width,), jnp.float32)
    gain_ffn_sum = jnp.zeros((model_width,), jnp.float32)
    operand_list = []
    back_buffer = jnp.zeros((batches, length, model_width), jnp.bfloat16)
    passed = jnp.zeros((length, model_width), jnp.bfloat16)
    for tick_index in range(tick_count):
        micro_index = tick_index - (sections - 1 - section_index)
        is_valid = (micro_index >= 0) & (micro_index < batches)
        micro_pick = jnp.clip(micro_index, 0, batches - 1)
        forward_tick = jnp.clip(micro_index + section_index, 0, tick_count - 1)
        stored = jax.tree.map(
            lambda member: lax.dynamic_index_in_dim(member, forward_tick, 0, keepdims=False),
            stacked,
        )
        if tick_index > 0:
            arrived = from_behind(passed, "section", -1)
        else:
            arrived = passed
        own_grad = lax.dynamic_index_in_dim(upstream, micro_pick, 0, keepdims=False)
        incoming = jnp.where(
            section_index == sections - 1, own_grad.astype(jnp.float32), arrived.astype(jnp.float32)
        )
        grad_stream, gain_terms, operands = layer_backward(
            incoming, weights, geometry_of(micro_pick), stored
        )
        passed = grad_stream.astype(jnp.bfloat16)
        back_buffer = jnp.where(
            is_valid,
            lax.dynamic_update_index_in_dim(back_buffer, passed, micro_pick, 0),
            back_buffer,
        )
        gain_attn_sum = gain_attn_sum + jnp.where(is_valid, gain_terms[0], 0.0)
        gain_ffn_sum = gain_ffn_sum + jnp.where(is_valid, gain_terms[1], 0.0)
        zero_value = jnp.zeros((), jnp.bfloat16)
        operands = tuple(
            (
                member if position % 2 == 0 else jnp.where(is_valid, member, zero_value)
                for position, member in enumerate(operands)
            )
        )
        operand_list.append(operands)
    columns = [
        jnp.concatenate([entry[position] for entry in operand_list], axis=0)
        for position in range(8)
    ]

    def weight_term(left, right):
        return jnp.einsum("sd,se->de", left, right, preferred_element_type=jnp.float32)

    qkv_sum = weight_term(columns[0], columns[1])
    out_sum = weight_term(columns[2], columns[3])
    gate_up_sum = weight_term(columns[4], columns[5])
    down_sum = weight_term(columns[6], columns[7])
    parts = (
        lax.psum_scatter(
            gain_attn_sum[None].astype(jnp.bfloat16), "shard", scatter_dimension=1, tiled=True
        ).astype(jnp.float32),
        lax.psum_scatter(
            qkv_sum[None].astype(jnp.bfloat16), "shard", scatter_dimension=1, tiled=True
        ).astype(jnp.float32),
        lax.psum_scatter(
            out_sum[None].astype(jnp.bfloat16), "shard", scatter_dimension=1, tiled=True
        ).astype(jnp.float32),
        lax.psum_scatter(
            gain_ffn_sum[None].astype(jnp.bfloat16), "shard", scatter_dimension=1, tiled=True
        ).astype(jnp.float32),
        lax.psum_scatter(
            gate_up_sum[None].astype(jnp.bfloat16), "shard", scatter_dimension=1, tiled=True
        ).astype(jnp.float32),
        lax.psum_scatter(
            down_sum[None].astype(jnp.bfloat16), "shard", scatter_dimension=1, tiled=True
        ).astype(jnp.float32),
    )
    gain_attn_out, qkv_out, out_out, gain_ffn_out, gate_up_out, down_out = (
        lax.psum(parts[0].astype(jnp.bfloat16), "replica").astype(jnp.float32),
        lax.psum(parts[1].astype(jnp.bfloat16), "replica").astype(jnp.float32),
        lax.psum(parts[2].astype(jnp.bfloat16), "replica").astype(jnp.float32),
        lax.psum(parts[3].astype(jnp.bfloat16), "replica").astype(jnp.float32),
        lax.psum(parts[4].astype(jnp.bfloat16), "replica").astype(jnp.float32),
        lax.psum(parts[5].astype(jnp.bfloat16), "replica").astype(jnp.float32),
    )
    return (
        outputs_buffer.reshape(1, batches * length, model_width),
        back_buffer.reshape(1, batches * length, model_width),
        gain_attn_out,
        qkv_out,
        out_out,
        gain_ffn_out,
        gate_up_out,
        down_out,
    )


def solution(mesh):
    return jax.shard_map(
        shards,
        mesh=mesh,
        in_specs=(
            P(("shard", "replica"), None),
            P(("shard", "replica"), None),
            P(("shard", "replica"), None),
            P("section", None),
            P("section", "shard", None),
            P("section", "shard", None),
            P("section", None),
            P("section", "shard", None),
            P("section", "shard", None),
        ),
        out_specs=(
            P("section", ("shard", "replica"), None),
            P("section", ("shard", "replica"), None),
            P("section", "shard"),
            P("section", "shard", None),
            P("section", "shard", None),
            P("section", "shard"),
            P("section", "shard", None),
            P("section", "shard", None),
        ),
        check_vma=False,
    )
```

profile of v0, /device:TPU:0, one launch (start us, length us, event | category | flops | bytes accessed | tf_op | source)
XLA Modules:
  0.0 428.8 jit_solution(769177574214147556)
XLA Ops:
  10.8 9.8 %all_gather.13 = bf16[1,576,576]{2,1,0:T(8,128)(2,1)S(1)} all-gather(bf16[1,144,576]{2,1,0:T(8,128)(2,1)S(1)} %copy-done.78), channel_id=1, replica_groups=mesh['section'=2,'shard'=4,'replica'=4] {'shard'}, dimensions={1}, use_global_device_ids=true | all-gather | bytes 829440 | tf_op jit(solution)/shard_map/all_gather | solution.py:236
  20.8 1.7 constant_dynamic-slice_fusion.5
  24.6 5.3 %all-gather.4.cloned.1.call-done = bf16[1,576,960]{2,1,0:T(8,128)(2,1)} async-done(((bf16[1,144,960]{2,1,0:T(8,128)(2,1)}), bf16[1,576,960]{2,1,0:T(8,128)(2,1)}) %all-gather.4.cloned.1.call-update) | async-done | bytes 1105936 | tf_op jit(solution)/shard_map/all_gather | solution.py:235
  29.8 2.0 fusion.66
  34.6 27.6 %all-gather.6.cloned.1.call-done = bf16[1,576,3072]{2,1,0:T(8,128)(2,1)} async-done(((bf16[1,144,3072]{2,1,0:T(8,128)(2,1)}), bf16[1,576,3072]{2,1,0:T(8,128)(2,1)}) %all-gather.6.cloned.1.call-update) | async-done | bytes 3538960 | tf_op jit(solution)/shard_map/all_gather | solution.py:237
  62.2 2.9 fusion.11
  65.1 19.4 %all-gather.8.cloned.1.call-done = bf16[1,1536,576]{1,2,0:T(8,128)(2,1)} async-done(((bf16[1,384,576]{1,2,0:T(8,128)(2,1)}), bf16[1,1536,576]{1,2,0:T(8,128)(2,1)}) %all-gather.8.cloned.1.call-update) | async-done | bytes 1769488 | tf_op jit(solution)/shard_map/all_gather | solution.py:238
  84.6 2.2 bitcast_dynamic-update-slice_fusion.1
  86.8 3.5 collective-permute-start
  90.6 3.2 collective-permute-done
  96.4 0.9 copy-done
  97.4 0.9 fusion.9
  98.5 1.2 copy-done.117
  100.5 4.6 %collective-permute-start.1 = (bf16[128,576]{0,1:T(8,128)(2,1)S(1)}, bf16[128,576]{0,1:T(8,128)(2,1)S(1)}, u32[]{:S(2)}, u32[]{:S(2)}) collective-permute-start(bf16[128,576]{0,1:T(8,128)(2,1)S(1)} %get-tuple-element.155), channel_id=1, source_target_pairs={{0,16},{1,17},{2,18},{3,19},{4,20},{5,21},{6,22},{7,23},{8,24},{9,... | collective-permute-start | bytes 442376 | tf_op jit(solution)/shard_map/ppermute | solution.py:22
  105.1 2.4 collective-permute-done.1
  107.6 0.8 fusion.161
  111.1 0.9 fusion.7
  112.2 1.7 copy-done.7
  114.5 1.6 dynamic-slice_bitcast_fusion
  116.2 0.9 copy-done.33
  117.8 1.1 fusion.5
  118.9 1.5 fusion.340
  120.5 0.8 broadcast_select_fusion.10
  124.8 1.5 fusion.282
  126.5 1.3 collective-permute-start.2
  128.0 5.6 %collective-permute-done.2 = bf16[128,576]{0,1:T(8,128)(2,1)S(1)} collective-permute-done((bf16[128,576]{0,1:T(8,128)(2,1)S(1)}, bf16[128,576]{0,1:T(8,128)(2,1)S(1)}, u32[]{:S(2)}, u32[]{:S(2)}) %collective-permute-start.2) | collective-permute-done | bytes 147488 | tf_op jit(solution)/shard_map/ppermute | solution.py:22
  134.4 1.7 fusion.206
  136.1 0.8 broadcast_select_fusion.9
  139.0 1.2 fusion.181
  140.4 1.5 collective-permute-start.3
  142.1 5.4 %collective-permute-done.3 = bf16[128,576]{0,1:T(8,128)(2,1)S(1)} collective-permute-done((bf16[128,576]{0,1:T(8,128)(2,1)S(1)}, bf16[128,576]{0,1:T(8,128)(2,1)S(1)}, u32[]{:S(2)}, u32[]{:S(2)}) %collective-permute-start.3) | collective-permute-done | bytes 147488 | tf_op jit(solution)/shard_map/ppermute | solution.py:22
  148.2 2.3 fusion.13
  150.5 8.7 %copy.97 = bf16[1,1536,576]{2,0,1:T(2,128)(2,1)} copy(bf16[1,1536,576]{1,2,0:T(8,128)(2,1)} %fusion.13) | data formatting | bytes 3538944
  159.2 3.7 copy.127
  163.0 1.8 broadcast_select_fusion.5
  164.8 1.2 pad_maximum_fusion.11
  166.2 0.8 dynamic-slice_bitcast_fusion.14
  169.0 1.8 fusion.198
  171.0 1.5 fusion.32
  172.8 1.1 convolution_bitcast_fusion
  176.0 1.8 fusion.31
  180.3 3.8 fusion
  185.7 2.1 fusion.190
  187.8 0.8 reshape_bitcast_fusion.2
  188.7 4.1 reduce-scatter.23.cloned.1.call-done
  192.8 1.5 reshape_bitcast_fusion
  194.4 1.8 copy.98
  196.2 22.7 %reduce-scatter.15.cloned.1.call-done = bf16[1,144,576]{2,1,0:T(8,128)(2,1)} async-done(((bf16[1,576,576]{2,1,0:T(8,128)(2,1)}), bf16[1,144,576]{2,1,0:T(8,128)(2,1)}) %reduce-scatter.15.cloned.1.call-update) | async-done | bytes 165904 | tf_op jit(solution)/shard_map/reduce_scatter | solution.py:335
  218.9 28.8 %reduce-scatter.13.cloned.1.call-done = bf16[1,144,960]{2,1,0:T(8,128)(2,1)} async-done(((bf16[1,576,960]{2,1,0:T(8,128)(2,1)}), bf16[1,144,960]{2,1,0:T(8,128)(2,1)}) %reduce-scatter.13.cloned.1.call-update) | async-done | bytes 276496 | tf_op jit(solution)/shard_map/reduce_scatter | solution.py:332
  247.7 43.2 %reduce-scatter.17.cloned.1.call-done = bf16[1,144,3072]{2,1,0:T(8,128)(2,1)} async-done(((bf16[1,576,3072]{2,1,0:T(8,128)(2,1)}), bf16[1,144,3072]{2,1,0:T(8,128)(2,1)}) %reduce-scatter.17.cloned.1.call-update) | async-done | bytes 884752 | tf_op jit(solution)/shard_map/reduce_scatter | solution.py:341
  290.9 2.3 fusion.101
  293.5 0.9 reshape.841
  294.4 1.1 fusion.226
  295.9 0.9 reshape.858
  296.8 16.2 %reduce-scatter.21.cloned.1.call-done = bf16[144,1]{1,0:T(8,128)(2,1)} async-done(((bf16[576,1]{1,0:T(8,128)(2,1)}), bf16[144,1]{1,0:T(8,128)(2,1)}) %reduce-scatter.21.cloned.1.call-update) | async-done | bytes 304
  312.9 0.8 copy.96
  313.8 21.3 %reduce-scatter.19.cloned.1.call-done = bf16[144,1]{1,0:T(8,128)(2,1)} async-done(((bf16[576,1]{1,0:T(8,128)(2,1)}), bf16[144,1]{1,0:T(8,128)(2,1)}) %reduce-scatter.19.cloned.1.call-update) | async-done | bytes 304
  335.0 0.8 copy.94
  335.9 11.9 %all-reduce = (bf16[1,144]{1,0:T(2,128)(2,1)S(1)}, bf16[1,144]{1,0:T(2,128)(2,1)S(1)}) all-reduce(bf16[1,144]{1,0:T(2,128)(2,1)S(1)} %copy.94, bf16[1,144]{1,0:T(2,128)(2,1)S(1)} %copy.96), channel_id=1, replica_groups=mesh['section'=2,'shard'=4,'replica'=4] {'replica'}, use_global_device_ids=true, to_apply=%region_26.27 | all-reduce | flops 288 | bytes 1152 | tf_op jit(solution)/shard_map/psum | solution.py:349
  348.9 67.1 %all-reduce.4.cloned.1.call-done = (bf16[1,144,960]{2,1,0:T(8,128)(2,1)}, bf16[1,144,576]{2,1,0:T(8,128)(2,1)}, bf16[1,144,3072]{2,1,0:T(8,128)(2,1)}, bf16[1,384,576]{1,2,0:T(8,128)(2,1)}) async-done(((bf16[1,144,960]{2,1,0:T(8,128)(2,1)}, bf16[1,144,576]{2,1,0:T(8,128)(2,1)}, bf16[1,144,3072]{2,1,0:T(8,128)(2,1)}, bf16[1,384,576]{1,2,0:T(8,128)(2,1)}), (bf16[1,144,960]{2,1,0:T(8,128)(2,1)}, ...) | async-done | bytes 1769488 | tf_op jit(solution)/shard_map/psum | solution.py:350
  415.9 1.9 convert_element_type.493
  417.9 1.7 convert_element_type.499
  419.6 1.0 convert_element_type.509
  420.5 1.4 convert_element_type.505
  (390 shorter events, 33.7 us)
Async XLA Ops:
  7.2 2.4 copy-start.18
  7.2 3.0 copy-start.100
  7.2 3.5 copy-start.63
  7.2 3.6 copy-start.78
  7.2 22.6 %all-gather.4.cloned.1.call-start = ((), (), s32[]{:S(2)}) async-start(), calls=%async_computation.6 | async-start | bytes 1474560 | tf_op jit(solution)/shard_map/all_gather | solution.py:235
  7.9 54.2 %all-gather.6.cloned.1.call-start = ((), (), s32[]{:S(2)}) async-start(), calls=%async_computation.7 | async-start | bytes 4423680 | tf_op jit(solution)/shard_map/all_gather | solution.py:237
  8.7 75.8 %all-gather.8.cloned.1.call-start = ((), (), s32[]{:S(2)}) async-start(), calls=%async_computation.8 | async-start | bytes 2211840 | tf_op jit(solution)/shard_map/all_gather | solution.py:238
  9.4 183.4 %reduce-scatter.23.cloned.1.call-start = ((), (), s32[]{:S(2)}) async-start(), calls=%async_computation.14 | async-start | bytes 2457600
  10.2 19.7 %copy-start.110 = (f32[128]{0:T(128)}, f32[128]{0:T(128)S(1)}, u32[]{:S(2)}) copy-start(f32[128]{0:T(128)S(1)} %get-tuple-element.133) | copy-start | bytes 1540
  10.8 13.0 %copy-start.107 = (f32[1,576]{1,0:T(1,128)S(1)}, f32[1,576]{1,0:T(1,128)}, u32[]{:S(2)}) copy-start(f32[1,576]{1,0:T(1,128)} %param.12) | copy-start | bytes 6916
  10.8 13.1 %copy-start.108 = (f32[1,576]{1,0:T(1,128)S(1)}, f32[1,576]{1,0:T(1,128)}, u32[]{:S(2)}) copy-start(f32[1,576]{1,0:T(1,128)} %param.15) | copy-start | bytes 6916
  20.6 12.8 %copy-start.1 = (bf16[1,576,576]{2,1,0:T(8,128)(2,1)}, bf16[1,576,576]{2,1,0:T(8,128)(2,1)S(1)}, u32[]{:S(2)}) copy-start(bf16[1,576,576]{2,1,0:T(8,128)(2,1)S(1)} %all_gather.13) | copy-start | bytes 1990660
  34.0 50.5 %copy-start.14 = (f32[128,576]{0,1:T(8,128)}, f32[128,576]{0,1:T(8,128)S(1)}, u32[]{:S(2)}) copy-start(f32[128,576]{0,1:T(8,128)S(1)} %get-tuple-element.147) | copy-start | bytes 884740
  34.6 30.5 %copy-start.113 = (f32[128]{0:T(128)}, f32[128]{0:T(128)S(1)}, u32[]{:S(2)}) copy-start(f32[128]{0:T(128)S(1)} %get-tuple-element.139) | copy-start | bytes 1540
  65.1 25.2 %copy-start.6 = (f32[128,3072]{1,0:T(8,128)}, f32[128,3072]{1,0:T(8,128)S(1)}, u32[]{:S(2)}) copy-start(f32[128,3072]{1,0:T(8,128)S(1)} %fusion.11) | copy-start | bytes 4718596
  86.8 7.1 %copy-start.8 = (bf16[1,576,960]{2,1,0:T(8,128)(2,1)S(1)}, bf16[1,576,960]{2,1,0:T(8,128)(2,1)}, u32[]{:S(2)}) copy-start(bf16[1,576,960]{2,1,0:T(8,128)(2,1)} %all-gather.4.cloned.1.call-done) | copy-start | bytes 3317764
  86.8 7.0 %collective-permute-start = (bf16[128,576]{0,1:T(8,128)(2,1)S(1)}, bf16[128,576]{0,1:T(8,128)(2,1)S(1)}, u32[]{:S(2)}, u32[]{:S(2)}) collective-permute-start(bf16[128,576]{0,1:T(8,128)(2,1)S(1)} %get-tuple-element.149), channel_id=1, source_target_pairs={{0,16},{1,17},{2,18},{3,19},{4,20},{5,21},{6,22},{7,23},{8,24},{9,... | collective-permute-start | bytes 442376 | tf_op jit(solution)/shard_map/ppermute | solution.py:22
  95.2 2.1 copy-start
  99.7 7.8 %copy-start.19 = (bf16[256,576]{0,1:T(8,128)(2,1)S(1)}, bf16[256,576]{0,1:T(8,128)(2,1)}, u32[]{:S(2)}) copy-start(bf16[256,576]{0,1:T(8,128)(2,1)} %param.9) | copy-start | bytes 884740
  99.7 7.8 %copy-start.111 = (f32[128]{0:T(128)S(1)}, f32[128]{0:T(128)}, u32[]{:S(2)}) copy-start(f32[128]{0:T(128)} %copy-done.110) | copy-start | bytes 1540
  100.5 8.7 %copy-start.34 = (bf16[2,128,576]{1,2,0:T(8,128)(2,1)}, bf16[2,128,576]{1,2,0:T(8,128)(2,1)S(1)}, u32[]{:S(2)}) copy-start(bf16[2,128,576]{1,2,0:T(8,128)(2,1)S(1)} %get-tuple-element.154) | copy-start | bytes 884740
  100.5 7.1 %collective-permute-start.1 = (bf16[128,576]{0,1:T(8,128)(2,1)S(1)}, bf16[128,576]{0,1:T(8,128)(2,1)S(1)}, u32[]{:S(2)}, u32[]{:S(2)}) collective-permute-start(bf16[128,576]{0,1:T(8,128)(2,1)S(1)} %get-tuple-element.155), channel_id=1, source_target_pairs={{0,16},{1,17},{2,18},{3,19},{4,20},{5,21},{6,22},{7,23},{8,24},{9,... | collective-permute-start | bytes 442376 | tf_op jit(solution)/shard_map/ppermute | solution.py:22
  105.1 4.1 copy-start.91
  105.1 4.1 copy-start.92
  110.5 8.4 %copy-start.12 = (f32[128,576]{0,1:T(8,128)}, f32[128,576]{0,1:T(8,128)S(1)}, u32[]{:S(2)}) copy-start(f32[128,576]{0,1:T(8,128)S(1)} %get-tuple-element.159) | copy-start | bytes 884740
  112.0 2.5 copy-start.4
  112.0 2.0 copy-start.7
  116.2 19.9 %copy-start.10 = (f32[3,128,576]{1,2,0:T(8,128)}, f32[3,128,576]{1,2,0:T(8,128)S(1)}, u32[]{:S(2)}) copy-start(f32[3,128,576]{1,2,0:T(8,128)S(1)} %pad_maximum_fusion.2) | copy-start | bytes 2654212
  121.7 15.6 %copy-start.52 = (bf16[3,128,3,64]{1,3,2,0:T(8,128)(2,1)}, bf16[3,128,3,64]{1,3,2,0:T(8,128)(2,1)S(1)}, u32[]{:S(2)}) copy-start(bf16[3,128,3,64]{1,3,2,0:T(8,128)(2,1)S(1)} %pad_maximum_fusion.16) | copy-start | bytes 442372
  122.1 16.6 %copy-start.31 = (bf16[3,128,3,64]{1,3,2,0:T(8,128)(2,1)}, bf16[3,128,3,64]{1,3,2,0:T(8,128)(2,1)S(1)}, u32[]{:S(2)}) copy-start(bf16[3,128,3,64]{1,3,2,0:T(8,128)(2,1)S(1)} %maximum_maximum_fusion.1) | copy-start | bytes 442372
  122.3 16.1 %copy-start.16 = (bf16[3,128,3,3,64]{1,4,3,2,0:T(8,128)(2,1)}, bf16[3,128,3,3,64]{1,4,3,2,0:T(8,128)(2,1)S(1)}, u32[]{:S(2)}) copy-start(bf16[3,128,3,3,64]{1,4,3,2,0:T(8,128)(2,1)S(1)} %maximum_maximum_fusion) | copy-start | bytes 1327108
  124.1 2.1 copy-start.75
  124.2 2.1 copy-start.45
  124.3 15.9 %copy-start.25 = (bf16[3,128,576]{1,2,0:T(8,128)(2,1)}, bf16[3,128,576]{1,2,0:T(8,128)(2,1)S(1)}, u32[]{:S(2)}) copy-start(bf16[3,128,576]{1,2,0:T(8,128)(2,1)S(1)} %pad_maximum_fusion.9) | copy-start | bytes 1327108
  126.3 7.3 %copy-start.24 = (bf16[1,128,576]{1,0,2:T(2,128)(2,1)S(1)}, bf16[1,128,576]{1,0,2:T(2,128)(2,1)}, u32[]{:S(2)}) copy-start(bf16[1,128,576]{1,0,2:T(2,128)(2,1)} %get-tuple-element.80) | copy-start | bytes 442372
  126.5 7.0 %collective-permute-start.2 = (bf16[128,576]{0,1:T(8,128)(2,1)S(1)}, bf16[128,576]{0,1:T(8,128)(2,1)S(1)}, u32[]{:S(2)}, u32[]{:S(2)}) collective-permute-start(bf16[128,576]{0,1:T(8,128)(2,1)S(1)} %get-tuple-element.39), channel_id=1, source_target_pairs={{16,0},{17,1},{18,2},{19,3},{20,4},{21,5},{22,6},{23,7},{24,8},{25... | collective-permute-start | bytes 442376 | tf_op jit(solution)/shard_map/ppermute | solution.py:22
  140.2 7.3 %copy-start.22 = (bf16[1,128,576]{1,0,2:T(2,128)(2,1)S(1)}, bf16[1,128,576]{1,0,2:T(2,128)(2,1)}, u32[]{:S(2)}) copy-start(bf16[1,128,576]{1,0,2:T(2,128)(2,1)} %get-tuple-element.79) | copy-start | bytes 442372
  140.4 7.0 %collective-permute-start.3 = (bf16[128,576]{0,1:T(8,128)(2,1)S(1)}, bf16[128,576]{0,1:T(8,128)(2,1)S(1)}, u32[]{:S(2)}, u32[]{:S(2)}) collective-permute-start(bf16[128,576]{0,1:T(8,128)(2,1)S(1)} %get-tuple-element.37), channel_id=1, source_target_pairs={{16,0},{17,1},{18,2},{19,3},{20,4},{21,5},{22,6},{23,7},{24,8},{25... | collective-permute-start | bytes 442376 | tf_op jit(solution)/shard_map/ppermute | solution.py:22
  162.9 56.0 %reduce-scatter.15.cloned.1.call-start = ((), (), s32[]{:S(2)}) async-start(), calls=%async_computation.10 | async-start | bytes 921600 | tf_op jit(solution)/shard_map/reduce_scatter | solution.py:335
  163.0 3.1 copy-start.43
  163.0 3.1 copy-start.48
  163.0 3.1 copy-start.49
  164.8 2.2 copy-start.47
  164.8 2.2 copy-start.72
  164.8 2.2 copy-start.77
  164.8 3.0 copy-start.118
  168.5 2.3 copy-start.58
  168.5 2.3 copy-start.60
  169.0 2.0 copy-start.79
  169.0 2.0 copy-start.80
  174.8 72.9 %reduce-scatter.13.cloned.1.call-start = ((), (), s32[]{:S(2)}) async-start(), calls=%async_computation.9 | async-start | bytes 1474560 | tf_op jit(solution)/shard_map/reduce_scatter | solution.py:332
  177.8 113.0 %reduce-scatter.17.cloned.1.call-start = ((), (), s32[]{:S(2)}) async-start(), calls=%async_computation.11 | async-start | bytes 4423680 | tf_op jit(solution)/shard_map/reduce_scatter | solution.py:341
  184.1 3.6 copy-start.103
  184.1 3.6 copy-start.105
  184.2 128.8 %reduce-scatter.21.cloned.1.call-start = ((), (), s32[]{:S(2)}) async-start(), calls=%async_computation.13 | async-start | bytes 184320
  185.6 149.4 %reduce-scatter.19.cloned.1.call-start = ((), (), s32[]{:S(2)}) async-start(), calls=%async_computation.12 | async-start | bytes 184320
  188.6 227.3 %all-reduce.4.cloned.1.call-start = ((), (), s32[]{:S(2)}) async-start(), calls=%async_computation.15 | async-start | bytes 3612672 | tf_op jit(solution)/shard_map/psum | solution.py:350
  194.4 96.5 %copy-start.5 = (f32[128,3072]{1,0:T(8,128)S(1)}, f32[128,3072]{1,0:T(8,128)}, u32[]{:S(2)}) copy-start(f32[128,3072]{1,0:T(8,128)} %copy-done.4) | copy-start | bytes 4718596
  194.4 96.5 %copy-start.13 = (f32[128,576]{0,1:T(8,128)S(1)}, f32[128,576]{0,1:T(8,128)}, u32[]{:S(2)}) copy-start(f32[128,576]{0,1:T(8,128)} %copy-done.12) | copy-start | bytes 884740
  194.4 96.5 %copy-start.35 = (bf16[2,128,576]{1,2,0:T(8,128)(2,1)S(1)}, bf16[2,128,576]{1,2,0:T(8,128)(2,1)}, u32[]{:S(2)}) copy-start(bf16[2,128,576]{1,2,0:T(8,128)(2,1)} %copy-done.34) | copy-start | bytes 884740
  290.9 3.5 copy-start.21
  290.9 3.5 copy-start.62
  415.9 3.6 copy-start.53
  415.9 4.6 %copy-start.36 = (bf16[1,144,3072]{2,1,0:T(8,128)(2,1)S(1)}, bf16[1,144,3072]{2,1,0:T(8,128)(2,1)}, u32[]{:S(2)}) copy-start(bf16[1,144,3072]{2,1,0:T(8,128)(2,1)} %get-tuple-element.24) | copy-start | bytes 2654212
  (69 other events, 85.0 us)
Sparse Core Ops, SparseCore 0:
  9.6 20.1 all-gather.3
  31.4 30.7 all-gather.5
  63.8 20.7 all-gather.7
  163.0 29.7 reduce-scatter.22
  196.0 22.9 reduce-scatter.14
  221.9 25.7 reduce-scatter.12
  250.4 40.3 reduce-scatter.16
  293.3 19.5 reduce-scatter.20
  315.4 19.6 reduce-scatter.18
  337.5 78.4 all-reduce.3
where the time goes:
time: 430 us; the launch traced here: 429 us
  waiting for transfers between devices  274 us (64%)
  matrix products  42.1 us (10%)
  local copies, waits for them, and re-layouts  38.4 us (9%)
  other arithmetic  24.7 us (6%)
  blocking collectives  21.7 us (5%)
  between operations  16.2 us (4%)
  starting transfers between devices  11.3 us (3%)
    psum x1, waiting for transfers between devices, shards(): lax.psum(parts[1].astype(jnp.bfloat16), 'replica').astype(jnp.float32)  67.1 us
    unnamed x13, waiting for transfers between devices  43.7 us
    reduce_scatter x1, waiting for transfers between devices, shards(): lax.psum_scatter(gate_up_sum[None].astype(jnp.bfloat16), 'shard', scatter...  43.2 us
    unnamed x246, local copies, waits for them, and re-layouts  29 us
    reduce_scatter x1, waiting for transfers between devices, shards(): lax.psum_scatter(qkv_sum[None].astype(jnp.bfloat16), 'shard', scatter_dim...  28.8 us
    all_gather x1, waiting for transfers between devices, shards(): lax.all_gather(gate_up_weight, 'shard', axis=1, tiled=True)  27.6 us
    reduce_scatter x1, waiting for transfers between devices, shards(): lax.psum_scatter(out_sum[None].astype(jnp.bfloat16), 'shard', scatter_dim...  22.7 us
    all_gather x1, waiting for transfers between devices, shards(): lax.all_gather(down_weight, 'shard', axis=1, tiled=True)  19.4 us
  transfers between devices with their start and end apart: 14, of which 14 were waited for; matrix products, arithmetic and copies ran while one was open for 11% of the time, Pallas kernels for 0%

commit v1 on v0

v1 whole, which is shorter than its diff:
```python
import functools
import math

import jax
import jax.numpy as jnp
from jax import lax
from jax.experimental import pallas as pl
from jax.experimental.pallas import tpu as pltpu
from jax.sharding import PartitionSpec as P

HEADS = 9
KV = 3
HD = 64
FF = 1536


norm_epsilon = 1e-05
rope_base = 100000.0
masked_value = -1e30


def geometry(segment_ids):
    count_cols = segment_ids.shape[-1]
    column = jnp.arange(count_cols, dtype=jnp.int32)
    previous = jnp.concatenate([segment_ids[..., :1], segment_ids[..., :-1]], axis=-1)
    doc_marks = jnp.where(segment_ids != previous, column, 0)
    doc_starts = lax.cummax(doc_marks, axis=doc_marks.ndim - 1)
    positions = (column - doc_starts).astype(jnp.float32)
    allowed = (segment_ids[..., :, None] == segment_ids[..., None, :]) & (
        column[:, None] >= column[None, :]
    )
    half_width = HD // 2
    frequency = jnp.exp(
        -(jnp.arange(half_width, dtype=jnp.float32) * (2.0 / HD)) * math.log(rope_base)
    )
    angles = positions[..., None] * frequency
    return (allowed, jnp.cos(angles), jnp.sin(angles))


def rotate(tensor, cosine_table, sine_table):
    half_width = tensor.shape[-1] // 2
    first_half = tensor[..., :half_width]
    second_half = tensor[..., half_width:]
    cosine_table = cosine_table[..., None, :]
    sine_table = sine_table[..., None, :]
    return jnp.concatenate(
        [
            first_half * cosine_table - second_half * sine_table,
            second_half * cosine_table + first_half * sine_table,
        ],
        axis=-1,
    )


def unrotate(tensor, cosine_table, sine_table):
    half_width = tensor.shape[-1] // 2
    first_half = tensor[..., :half_width]
    second_half = tensor[..., half_width:]
    cosine_table = cosine_table[..., None, :]
    sine_table = sine_table[..., None, :]
    return jnp.concatenate(
        [
            first_half * cosine_table + second_half * sine_table,
            second_half * cosine_table - first_half * sine_table,
        ],
        axis=-1,
    )


def masked_scores(query_rows, key_rows, allowed):
    scores = jnp.einsum(
        "gqkrd,gtkd->gkrqt", query_rows, key_rows, preferred_element_type=jnp.float32
    ) * HD ** (-0.5)
    return jnp.where(allowed[:, None, None], scores, masked_value)


def norm_back(residual, stream, inverse, gain_row, grad_out):
    grad_gain = jnp.sum(grad_out * stream * inverse, axis=0)
    grad_hat = grad_out * gain_row
    inner = jnp.mean(grad_hat * stream, axis=-1, keepdims=True)
    return (residual + inverse * (grad_hat - stream * inverse * inverse * inner), grad_gain)


def layer_forward(layer_in, weights, geom):
    gain_attn, qkv_layer, out_layer, gain_ffn, gate_up_layer, down_layer = weights
    allowed, cosine_table, sine_table = geom
    groups, length = allowed.shape[:2]
    stream = layer_in.astype(jnp.float32)
    inv_attn = lax.rsqrt(jnp.mean(stream * stream, axis=-1, keepdims=True) + norm_epsilon)
    normed = (stream * inv_attn * gain_attn).astype(jnp.bfloat16)
    projected = jnp.dot(normed, qkv_layer, preferred_element_type=jnp.float32)
    projected = projected.reshape(groups, length, HEADS + 2 * KV, HD)
    query_rows = projected[:, :, :HEADS]
    key_rows = projected[:, :, HEADS : HEADS + KV]
    value_rows = projected[:, :, HEADS + KV :].astype(jnp.bfloat16)
    query_rows = (
        rotate(query_rows, cosine_table, sine_table)
        .astype(jnp.bfloat16)
        .reshape(groups, length, KV, HEADS // KV, HD)
    )
    key_rows = rotate(key_rows, cosine_table, sine_table).astype(jnp.bfloat16)
    scores = masked_scores(query_rows, key_rows, allowed)
    row_max = jnp.max(scores, axis=-1, keepdims=True)
    row_exp = jnp.exp(scores - row_max)
    row_sum = jnp.sum(row_exp, axis=-1, keepdims=True)
    attn_probs = row_exp / row_sum
    attended = jnp.einsum(
        "gkrqt,gtkd->gqkrd",
        attn_probs.astype(jnp.bfloat16),
        value_rows,
        preferred_element_type=jnp.float32,
    )
    attended = attended.reshape(groups * length, HEADS * HD).astype(jnp.bfloat16)
    middle = stream + jnp.dot(attended, out_layer, preferred_element_type=jnp.float32)
    inv_ffn = lax.rsqrt(jnp.mean(middle * middle, axis=-1, keepdims=True) + norm_epsilon)
    ffn_normed = (middle * inv_ffn * gain_ffn).astype(jnp.bfloat16)
    gate_up = jnp.dot(ffn_normed, gate_up_layer, preferred_element_type=jnp.float32)
    hidden = (jax.nn.silu(gate_up[:, :FF]) * gate_up[:, FF:]).astype(jnp.bfloat16)
    result = middle + jnp.dot(hidden, down_layer, preferred_element_type=jnp.float32)
    stored = (
        stream,
        inv_attn,
        normed,
        query_rows,
        key_rows,
        value_rows,
        attn_probs,
        attended,
        middle,
        inv_ffn,
        ffn_normed,
        gate_up,
        hidden,
    )
    return (result, stored)


def layer_backward(incoming, weights, geom, stored):
    gain_attn, qkv_layer, out_layer, gain_ffn, gate_up_layer, down_layer = weights
    allowed, cosine_table, sine_table = geom
    groups, length = allowed.shape[:2]
    (
        stream,
        inv_attn,
        normed,
        query_rows,
        key_rows,
        value_rows,
        attn_probs,
        attended,
        middle,
        inv_ffn,
        ffn_normed,
        gate_up,
        hidden,
    ) = stored
    out_rounded = incoming.astype(jnp.bfloat16)
    grad_hidden = jnp.einsum(
        "sd,fd->sf", out_rounded, down_layer, preferred_element_type=jnp.float32
    )
    gate_part = gate_up[:, :FF]
    up_part = gate_up[:, FF:]
    gate_sigmoid = jax.nn.sigmoid(gate_part)
    gate_silu = gate_part * gate_sigmoid
    grad_gate = grad_hidden * up_part * gate_sigmoid * (1.0 + gate_part * (1.0 - gate_sigmoid))
    grad_gu = jnp.concatenate([grad_gate, grad_hidden * gate_silu], axis=-1).astype(jnp.bfloat16)
    grad_fnorm = jnp.einsum("se,de->sd", grad_gu, gate_up_layer, preferred_element_type=jnp.float32)
    grad_middle, grad_gain_ffn = norm_back(incoming, middle, inv_ffn, gain_ffn, grad_fnorm)
    mid_rounded = grad_middle.astype(jnp.bfloat16)
    grad_att = jnp.einsum("sd,cd->sc", mid_rounded, out_layer, preferred_element_type=jnp.float32)
    grad_att = grad_att.astype(jnp.bfloat16).reshape(groups, length, KV, HEADS // KV, HD)
    grad_values = jnp.einsum(
        "gkrqt,gqkrd->gtkd",
        attn_probs.astype(jnp.bfloat16),
        grad_att,
        preferred_element_type=jnp.float32,
    )
    grad_probs = jnp.einsum(
        "gqkrd,gtkd->gkrqt", grad_att, value_rows, preferred_element_type=jnp.float32
    )
    inner = jnp.sum(attn_probs * grad_probs, axis=-1, keepdims=True)
    grad_scores = (attn_probs * (grad_probs - inner)).astype(jnp.bfloat16)
    grad_query = jnp.einsum(
        "gkrqt,gtkd->gqkrd", grad_scores, key_rows, preferred_element_type=jnp.float32
    ) * HD ** (-0.5)
    grad_keys = jnp.einsum(
        "gkrqt,gqkrd->gtkd", grad_scores, query_rows, preferred_element_type=jnp.float32
    ) * HD ** (-0.5)
    grad_query = unrotate(
        grad_query.reshape(groups, length, HEADS, HD), cosine_table, sine_table
    ).reshape(groups * length, HEADS * HD)
    grad_keys = unrotate(grad_keys, cosine_table, sine_table).reshape(groups * length, KV * HD)
    grad_projected = jnp.concatenate(
        [grad_query, grad_keys, grad_values.reshape(groups * length, KV * HD)], axis=-1
    ).astype(jnp.bfloat16)
    grad_normed = jnp.einsum(
        "se,de->sd", grad_projected, qkv_layer, preferred_element_type=jnp.float32
    )
    grad_stream, grad_gain_attn = norm_back(grad_middle, stream, inv_attn, gain_attn, grad_normed)
    operands = (
        (hidden, out_rounded),
        (ffn_normed, grad_gu),
        (attended, mid_rounded),
        (normed, grad_projected),
    )
    return (grad_stream, (grad_gain_attn, grad_gain_ffn), operands)


GAIN_ROWS = 16
MESH_ID = pl.DeviceIdType.MESH


def split_pieces(shapes):
    pieces = []
    for array, (rows, columns) in enumerate(shapes):
        row_step = 128 if rows > 144 and rows % 128 == 0 else rows
        column_step = 512 if columns > 1024 else columns
        for row in range(0, rows, row_step):
            for column in range(0, columns, column_step):
                pieces.append((array, row, row_step, column, column_step))
    return pieces


def reduce_kernel(pieces, replicas, *refs):
    count = len(pieces) + 1
    lefts, rights, gain_ref = refs[0:4], refs[4:8], refs[8]
    outs, gain_out = refs[9:13], refs[13]
    scratch = refs[14:]
    groups = [scratch[k * count : (k + 1) * count] for k in range(8)]
    send_a, recv_a, keep_a, send_b, recv_b, send_c, recv_c, recv_x = groups
    totals = scratch[8 * count : 9 * count]
    sems = scratch[9 * count :]
    a_out, a_in, b_out, b_in, c_out, c_in, x_out, x_in = sems

    shard = lax.axis_index("shard")
    place = lax.axis_index("replica")
    core = shard % 2
    row_y = shard // 2
    sibling = row_y * 2 + (1 - core)
    across = (1 - row_y) * 2 + core
    half = replicas // 2
    is_left = place < half
    inward = jnp.where(is_left, place + 1, place - 1)
    outward = jnp.where(is_left, place - 1, place + 1)
    is_middle = (place == half - 1) | (place == half)
    has_outer = (place > 0) & (place < replicas - 1)

    barrier = pltpu.get_barrier_semaphore()
    for peer in (sibling, across):
        pl.semaphore_signal(barrier, inc=1, device_id={"shard": peer}, device_id_type=MESH_ID)
    pl.semaphore_signal(barrier, inc=1, device_id={"replica": inward}, device_id_type=MESH_ID)

    @pl.when(has_outer)
    def _():
        pl.semaphore_signal(barrier, inc=1, device_id={"replica": outward}, device_id_type=MESH_ID)

    pl.semaphore_wait(barrier, jnp.where(has_outer, 4, 3))

    def copy(source, target, out_sem, in_sem, device):
        return pltpu.make_async_remote_copy(
            src_ref=source,
            dst_ref=target,
            send_sem=out_sem,
            recv_sem=in_sem,
            device_id=device,
            device_id_type=MESH_ID,
        )

    def copy_a(p):
        return copy(send_a[p], recv_a[p], a_out.at[p], a_in.at[p], {"shard": sibling})

    def copy_b(p):
        return copy(send_b[p], recv_b[p], b_out.at[p], b_in.at[p], {"shard": across})

    def copy_c(p):
        return copy(send_c[p], recv_c[p], c_out.at[p], c_in.at[p], {"replica": inward})

    def copy_middle(p):
        return copy(send_c[p], recv_x[p], c_out.at[p], x_in.at[p], {"replica": inward})

    def copy_x(p):
        return copy(totals[p], recv_x[p], x_out.at[p], x_in.at[p], {"replica": outward})

    def term(p, owner):
        if p == count - 1:
            return gain_ref[owner]
        array, row, rows, column, columns = pieces[p]
        return jnp.dot(
            lefts[array][owner, row : row + rows, :],
            rights[array][:, column : column + columns],
            preferred_element_type=jnp.float32,
        )

    def stage_a(p):
        for y in range(2):
            send_a[p][y] = term(p, 2 * y + (1 - core)).astype(jnp.bfloat16)
        copy_a(p).start()
        for y in range(2):
            keep_a[p][y] = term(p, 2 * y + core)

    def stage_b(p):
        copy_a(p).wait_recv()
        other = 1 - row_y
        send_b[p][...] = (keep_a[p][other] + recv_a[p][other].astype(jnp.float32)).astype(
            jnp.bfloat16
        )
        copy_b(p).start()

    def stage_c(p):
        copy_b(p).wait_recv()
        keep_a[p][0] = (
            keep_a[p][row_y]
            + recv_a[p][row_y].astype(jnp.float32)
            + recv_b[p][...].astype(jnp.float32)
        )

        @pl.when(has_outer)
        def _():
            copy_c(p).wait_recv()
            keep_a[p][0] = keep_a[p][0] + recv_c[p][...].astype(jnp.float32)

        send_c[p][...] = keep_a[p][0].astype(jnp.bfloat16)

        @pl.when(is_middle)
        def _():
            copy_middle(p).start()

        @pl.when(jnp.logical_not(is_middle))
        def _():
            copy_c(p).start()

    def stage_d(p):
        copy_x(p).wait_recv()

        @pl.when(is_middle)
        def _():
            totals[p][...] = (
                send_c[p][...].astype(jnp.float32) + recv_x[p][...].astype(jnp.float32)
            ).astype(jnp.bfloat16)

        @pl.when(jnp.logical_not(is_middle))
        def _():
            totals[p][...] = recv_x[p][...]

        @pl.when(has_outer)
        def _():
            copy_x(p).start()

        total = totals[p][...].astype(jnp.float32)
        if p == count - 1:
            gain_out[...] = total
        else:
            array, row, rows, column, columns = pieces[p]
            outs[array][row : row + rows, column : column + columns] = total

    for step in range(count + 4):
        if step < count:
            stage_a(step)
        if 0 <= step - 1 < count:
            stage_b(step - 1)
        if 0 <= step - 2 < count:
            stage_c(step - 2)
        if 0 <= step - 4 < count:
            stage_d(step - 4)
    for p in range(count):
        copy_a(p).wait_send()
        copy_b(p).wait_send()
        copy_c(p).wait_send()

        @pl.when(has_outer)
        def _(p=p):
            copy_x(p).wait_send()


def reduce_gradients(operands, gains, replicas):
    owners = lax.axis_size("shard")
    lefts, rights, shapes = [], [], []
    for left, right in operands:
        tokens, rows = left.shape
        lefts.append(left.T.reshape(owners, rows // owners, tokens))
        rights.append(right)
        shapes.append((rows // owners, right.shape[1]))
    width = gains[0].shape[0] // owners
    packed = jnp.stack([gain.reshape(owners, width) for gain in gains], axis=1)
    packed = jnp.pad(packed, ((0, 0), (0, GAIN_ROWS - 2), (0, 256 - width)))
    pieces = split_pieces(shapes)
    extents = [(rows, columns) for _, _, rows, _, columns in pieces] + [(GAIN_ROWS, 256)]
    low, full = jnp.bfloat16, jnp.float32
    scratch = []
    for lead, kind in (
        ((2,), low),
        ((2,), low),
        ((2,), full),
        ((), low),
        ((), low),
        ((), low),
        ((), low),
        ((), low),
        ((), low),
    ):
        scratch += [pltpu.VMEM(lead + extent, kind) for extent in extents]
    scratch += [pltpu.SemaphoreType.DMA((len(extents),))] * 8
    vmem = pl.BlockSpec(memory_space=pltpu.VMEM)
    flops = sum(2 * left.shape[0] * left.shape[1] * right.shape[1] for left, right in operands)
    results = pl.pallas_call(
        functools.partial(reduce_kernel, pieces, replicas),
        out_shape=[jax.ShapeDtypeStruct(shape, full) for shape in shapes]
        + [jax.ShapeDtypeStruct((GAIN_ROWS, 256), full)],
        in_specs=[vmem] * 9,
        out_specs=[vmem] * 5,
        scratch_shapes=scratch,
        compiler_params=pltpu.CompilerParams(
            collective_id=1, has_side_effects=True, vmem_limit_bytes=58 * 2**20
        ),
        cost_estimate=pl.CostEstimate(flops=flops, bytes_accessed=2 * 2**20, transcendentals=0),
    )(*lefts, *rights, packed)
    gain_rows = results[4]
    return results[:4], [gain_rows[i : i + 1, :width] for i in range(2)]


def from_behind(block, axis, distance):
    devices = range(lax.axis_size(axis))
    route = [(i - distance, i) for i in devices if i - distance in devices]
    return lax.ppermute(block, axis, route)


def shards(
    inputs,
    segments,
    cotangent,
    attn_gain,
    qkv_weight,
    out_weight,
    ffn_gain,
    gate_up_weight,
    down_weight,
):
    sections = lax.axis_size("section")
    section_index = lax.axis_index("section")
    qkv_full, out_full, gate_up_full, down_full = (
        lax.all_gather(qkv_weight[0], "shard", axis=0, tiled=True),
        lax.all_gather(out_weight[0], "shard", axis=0, tiled=True),
        lax.all_gather(gate_up_weight[0], "shard", axis=0, tiled=True),
        lax.all_gather(down_weight[0], "shard", axis=0, tiled=True),
    )
    weights = (attn_gain[0], qkv_full, out_full, ffn_gain[0], gate_up_full, down_full)
    geom = geometry(segments)
    layer_in = inputs
    for tick in range(sections):
        if tick > 0:
            arrived = from_behind(outgoing, "section", 1)
            layer_in = jnp.where(section_index == 0, inputs, arrived)
        result, stored = layer_forward(layer_in, weights, geom)
        outgoing = result.astype(jnp.bfloat16)
    incoming = cotangent
    for tick in range(sections):
        if tick > 0:
            arrived = from_behind(passed, "section", -1)
            incoming = jnp.where(section_index == sections - 1, cotangent, arrived)
        grad_stream, gain_terms, operands = layer_backward(
            incoming.astype(jnp.float32), weights, geom, stored
        )
        passed = grad_stream.astype(jnp.bfloat16)
    sums, gain_sums = reduce_gradients(operands, gain_terms, lax.axis_size("replica"))
    down_sum, gate_up_sum, out_sum, qkv_sum = sums
    return (
        outgoing[None],
        passed[None],
        gain_sums[0],
        qkv_sum[None],
        out_sum[None],
        gain_sums[1],
        gate_up_sum[None],
        down_sum[None],
    )


def solution(mesh):
    return jax.shard_map(
        shards,
        mesh=mesh,
        in_specs=(
            P(("shard", "replica"), None),
            P(("shard", "replica"), None),
            P(("shard", "replica"), None),
            P("section", None),
            P("section", "shard", None),
            P("section", "shard", None),
            P("section", None),
            P("section", "shard", None),
            P("section", "shard", None),
        ),
        out_specs=(
            P("section", ("shard", "replica"), None),
            P("section", ("shard", "replica"), None),
            P("section", "shard"),
            P("section", "shard", None),
            P("section", "shard", None),
            P("section", "shard"),
            P("section", "shard", None),
            P("section", "shard", None),
        ),
        check_vma=False,
    )
```

time: 430 us -> 301 us (0.70)
  waiting for transfers between devices: 274 us -> 70 us
  Pallas kernels: 0 us -> 124 us
  other arithmetic: 24.7 us -> 10.2 us
  blocking collectives: 21.7 us -> 9.81 us
  local copies, waits for them, and re-layouts: 38.4 us -> 28.7 us
  starting transfers between devices: 11.3 us -> 5.31 us
  matrix products: 42.1 us -> 36.4 us
    pallas_call x0 -> x1, Pallas kernels: none -> 124 us  [reduce_gradients(): pl.pallas_call(functools.partial(reduce_kernel, pieces, replicas), out_sh...]
    reduce_scatter x3 -> x0, waiting for transfers between devices: 94.7 us -> none  [the longest x1 43.2 us: shards(): lax.psum_scatter(gate_up_sum[None].astype(jnp.bfloat16), 'shard', scatter...]
    psum x1 -> x0, waiting for transfers between devices: 67.1 us -> none  [shards(): lax.psum(parts[1].astype(jnp.bfloat16), 'replica').astype(jnp.float32)]
    unnamed x13 -> x3, waiting for transfers between devices: 43.7 us -> 2.06 us
    psum x1 -> x0, blocking collectives: 11.9 us -> none  [shards(): lax.psum(parts[0].astype(jnp.bfloat16), 'replica').astype(jnp.float32)]
    unnamed x246 -> x167, local copies, waits for them, and re-layouts: 29 us -> 18.9 us
    dot_general x25 -> x10, matrix products: 15.9 us -> 6.58 us  [the longest x2 2.35 us: layer_forward(): jnp.einsum('gkrqt,gtkd->gqkrd', attn_probs.astype(jnp.bfloat16), value_ro...]
    select_n x15 -> x1, other arithmetic: 7.76 us -> 1.01 us  [shards(): incoming = jnp.where(section_index == sections - 1, cotangent, arrived)]
  transfers between devices with their start and end apart: 14 -> 5, of which waited for: 14 -> 5; matrix products, arithmetic and copies ran while one was open for 11% -> 5% of each run, Pallas kernels for 0% -> 0%
where the time goes in v1:
time: 301 us; the launch traced here: 300 us
  Pallas kernels  124 us (41%)
  waiting for transfers between devices  70 us (23%)
  matrix products  36.4 us (12%)
  local copies, waits for them, and re-layouts  28.7 us (10%)
  between operations  15 us (5%)
  other arithmetic  10.2 us (3%)
  blocking collectives  9.81 us (3%)
  starting transfers between devices  5.31 us (2%)
    pallas_call x1, Pallas kernels, reduce_gradients(): pl.pallas_call(functools.partial(reduce_kernel, pieces, replicas), out_sh...  124 us
    all_gather x1, waiting for transfers between devices, shards(): lax.all_gather(gate_up_weight[0], 'shard', axis=0, tiled=True)  26.4 us
    unnamed x167, local copies, waits for them, and re-layouts  18.9 us
    all_gather x1, waiting for transfers between devices, shards(): lax.all_gather(down_weight[0], 'shard', axis=0, tiled=True)  18.7 us
    ppermute x2, waiting for transfers between devices, from_behind(): return lax.ppermute(block, axis, route)  13.6 us
    all_gather x1, blocking collectives, shards(): lax.all_gather(out_weight[0], 'shard', axis=0, tiled=True)  9.81 us
    all_gather x1, waiting for transfers between devices, shards(): lax.all_gather(qkv_weight[0], 'shard', axis=0, tiled=True)  9.24 us
  transfers between devices with their start and end apart: 5, of which 5 were waited for; matrix products, arithmetic and copies ran while one was open for 5% of the time, Pallas kernels for 0%

profile of v1, /device:TPU:0, one launch (start us, length us, event | category | flops | bytes accessed | tf_op | source)
XLA Modules:
  0.0 299.7 jit_solution(584507168855190309)
XLA Ops:
  7.3 0.7 all-gather.8.cloned.1.call-update
  8.0 0.7 all-gather.10.cloned.1.call-update
  8.7 0.7 all-gather.12.cloned.1.call-update
  10.8 9.8 %all-gather.1 = bf16[1,576,576]{2,1,0:T(8,128)(2,1)S(1)} all-gather(bf16[1,144,576]{2,1,0:T(8,128)(2,1)S(1)} %copy-done.62), channel_id=3, replica_groups=mesh['section'=2,'shard'=4,'replica'=4] {'shard'}, dimensions={1}, use_global_device_ids=true | all-gather | bytes 829440 | tf_op jit(solution)/shard_map/all_gather | solution.py:442
  20.6 9.2 %all-gather.8.cloned.1.call-done = bf16[1,576,960]{2,1,0:T(8,128)(2,1)} async-done(((bf16[1,144,960]{2,1,0:T(8,128)(2,1)}), bf16[1,576,960]{2,1,0:T(8,128)(2,1)}) %all-gather.8.cloned.1.call-update) | async-done | bytes 1105936 | tf_op jit(solution)/shard_map/all_gather | solution.py:441
  29.8 2.0 fusion.55
  31.8 0.5 reshape.177
  32.9 0.6 fusion.161
  33.4 0.7 fusion.57
  34.4 1.3 multiply_reduce_fusion.6
  35.8 26.4 %all-gather.10.cloned.1.call-done = bf16[1,576,3072]{2,1,0:T(8,128)(2,1)} async-done(((bf16[1,144,3072]{2,1,0:T(8,128)(2,1)}), bf16[1,576,3072]{2,1,0:T(8,128)(2,1)}) %all-gather.10.cloned.1.call-update) | async-done | bytes 3538960 | tf_op jit(solution)/shard_map/all_gather | solution.py:443
  62.2 3.6 %fusion.8 = f32[256,3072]{1,0:T(8,128)S(1)} fusion(bf16[1,576,3072]{2,1,0:T(8,128)(2,1)} %all-gather.10.cloned.1.call-done, f32[256,576]{1,0:T(8,128)} %get-tuple-element.77, f32[576]{0:T(1024)S(1)} %reduce.1, f32[256]{0:T(256)S(1)} %add_rsqrt_fusion.2), kind=kOutput, calls=%fused_computation.8 | convolution fusion | flops 906412032 | bytes 7277824 | tf_op jit(solution)/shard_map/dot_general | solution.py:117
  65.8 18.7 %all-gather.12.cloned.1.call-done = bf16[1,1536,576]{1,2,0:T(8,128)(2,1)} async-done(((bf16[1,384,576]{1,2,0:T(8,128)(2,1)}), bf16[1,1536,576]{1,2,0:T(8,128)(2,1)}) %all-gather.12.cloned.1.call-update) | async-done | bytes 1769488 | tf_op jit(solution)/shard_map/all_gather | solution.py:444
  84.5 3.2 %fusion.44 = bf16[256,576]{1,0:T(8,128)(2,1)} fusion(f32[256,576]{1,0:T(8,128)} %get-tuple-element.77, bf16[1,1536,576]{1,2,0:T(8,128)(2,1)} %all-gather.12.cloned.1.call-done, f32[256,3072]{1,0:T(8,128)S(1)} %fusion.8), kind=kOutput, calls=%fused_computation.58 | convolution fusion | flops 455639040 | bytes 5799936 | tf_op jit(solution)/shard_map/dot_general | solution.py:119
  87.7 3.7 %collective-permute-start = (bf16[256,576]{1,0:T(8,128)(2,1)}, bf16[256,576]{1,0:T(8,128)(2,1)S(1)}, u32[]{:S(2)}, u32[]{:S(2)}) collective-permute-start(bf16[256,576]{1,0:T(8,128)(2,1)} %fusion.44), channel_id=1, source_target_pairs={{0,16},{1,17},{2,18},{3,19},{4,20},{5,21},{6,22},{7,23},{8,24},{9,... | collective-permute-start | bytes 884744 | tf_op jit(solution)/shard_map/ppermute | solution.py:424
  91.4 1.9 copy.91
  93.2 5.6 %collective-permute-done = bf16[256,576]{1,0:T(8,128)(2,1)S(1)} collective-permute-done((bf16[256,576]{1,0:T(8,128)(2,1)}, bf16[256,576]{1,0:T(8,128)(2,1)S(1)}, u32[]{:S(2)}, u32[]{:S(2)}) %collective-permute-start) | collective-permute-done | bytes 294944 | tf_op jit(solution)/shard_map/ppermute | solution.py:424
  99.1 0.7 copy-done.10
  99.8 0.7 fusion.53
  100.5 0.5 reshape.178
  101.1 0.7 slice.129
  102.3 2.2 fusion.164
  104.5 1.7 fusion.58
  106.6 0.6 multiply_reduce_fusion.5
  107.2 1.4 fusion.6
  109.0 1.3 multiply_convert_fusion.3
  110.6 1.5 multiply_reduce_fusion.4
  112.1 0.8 copy-done.24
  113.0 1.3 convolution_convert_fusion.3
  114.2 1.7 reshape.179
  116.0 1.8 fusion.66
  118.5 0.6 copy-done.28
  120.4 0.5 add_convert_fusion.1
  121.6 0.7 fusion.90
  123.0 1.1 fusion.80
  124.1 1.5 collective-permute-start.1
  125.6 1.7 copy.217
  127.4 8.0 %collective-permute-done.1 = bf16[256,576]{1,0:T(8,128)(2,1)} collective-permute-done((bf16[256,576]{1,0:T(8,128)(2,1)}, bf16[256,576]{1,0:T(8,128)(2,1)}, u32[]{:S(2)}, u32[]{:S(2)}) %collective-permute-start.1) | collective-permute-done | bytes 294944 | tf_op jit(solution)/shard_map/ppermute | solution.py:424
  135.4 1.0 broadcast_select_fusion.refs_4_
  136.4 4.5 %multiply_convert_fusion.1 = (bf16[256,1536]{1,0:T(8,128)(2,1)S(1)}, bf16[256,1536]{1,0:T(8,128)(2,1)S(1)}, bf16[256,1536]{1,0:T(8,128)(2,1)}) fusion(f32[256,3072]{1,0:T(8,128)} %copy-done.19, bf16[256,576]{1,0:T(8,128)(2,1)S(1)} %broadcast_select_fusion.refs_4_, bf16[1,1536,576]{1,2,0:T(8,128)(2,1)} %all-gather.12.cloned.1.call-done), kind=kOutput, calls=%fused_computation.25 | convolution fusion | flops 458883072 | bytes 7569408 | tf_op jit(solution)/shard_map/sd,fd->sf/dot_general | solution.py:158
  140.9 1.4 pad_maximum_fusion.refs_5_
  142.3 2.1 multiply_reduce_fusion.2
  144.7 0.6 copy-done.22
  145.3 0.5 copy-done.7
  145.8 0.4 convolution_convert_fusion.2
  146.7 0.5 copy-done.64
  147.9 0.6 copy-done.29
  149.3 0.5 copy-done.4
  150.0 0.8 fusion.47
  150.9 0.9 copy.111
  151.8 1.2 copy.138
  153.8 0.5 add_convert_fusion
  155.7 1.5 fusion.93
  157.3 1.6 fusion.154
  158.8 0.9 copy.106
  159.7 0.9 copy.112
  160.6 0.9 copy.107
  161.5 0.6 select_maximum_fusion.refs_8_
  162.1 124.4 %shard_map.152 = (f32[384,576]{1,0:T(8,128)}, f32[144,3072]{1,0:T(8,128)}, f32[144,576]{1,0:T(8,128)}, f32[144,960]{1,0:T(8,128)}, f32[16,256]{1,0:T(8,128)}) custom-call(bf16[4,384,256]{2,1,0:T(8,128)(2,1)} %bitcast.296, bf16[4,144,256]{2,1,0:T(8,128)(2,1)} %bitcast.307, bf16[4,144,256]{2,1,0:T(8,128)(2,1)} %bitcast.306, bf16[4,144,256]{2,1,0:T(8,128)(2,1)} %bitcast.308, ...), custom_call_target="tpu_custom_call" | custom-call | flops 1811939328 | bytes 2097152 | tf_op jit(solution)/shard_map/pallas_call | solution.py:405
  286.5 1.4 fusion.160
  287.9 2.6 copy.113
  290.4 0.8 copy.223
  291.3 0.7 copy.224
  292.0 1.2 copy.225
  (218 shorter events, 11.5 us)
Async XLA Ops:
  7.2 2.3 copy-start.69
  7.2 2.8 copy-start.59
  7.2 3.4 %copy-start.73 = (f32[1,576]{1,0:T(1,128)S(1)}, f32[1,576]{1,0:T(1,128)}, u32[]{:S(2)}) copy-start(f32[1,576]{1,0:T(1,128)} %param.15) | copy-start | bytes 6916
  7.2 3.4 %copy-start.74 = (f32[1,576]{1,0:T(1,128)S(1)}, f32[1,576]{1,0:T(1,128)}, u32[]{:S(2)}) copy-start(f32[1,576]{1,0:T(1,128)} %param.12) | copy-start | bytes 6916
  7.2 3.5 %copy-start.62 = (bf16[1,144,576]{2,1,0:T(8,128)(2,1)S(1)}, bf16[1,144,576]{2,1,0:T(8,128)(2,1)}, u32[]{:S(2)}) copy-start(bf16[1,144,576]{2,1,0:T(8,128)(2,1)} %param.14) | copy-start | bytes 497668
  7.2 22.6 %all-gather.8.cloned.1.call-start = ((), (), s32[]{:S(2)}) async-start(), calls=%async_computation | async-start | bytes 1474560 | tf_op jit(solution)/shard_map/all_gather | solution.py:441
  8.0 54.2 %all-gather.10.cloned.1.call-start = ((), (), s32[]{:S(2)}) async-start(), calls=%async_computation.1 | async-start | bytes 4423680 | tf_op jit(solution)/shard_map/all_gather | solution.py:443
  8.7 75.8 %all-gather.12.cloned.1.call-start = ((), (), s32[]{:S(2)}) async-start(), calls=%async_computation.2 | async-start | bytes 2211840 | tf_op jit(solution)/shard_map/all_gather | solution.py:444
  10.0 23.4 %copy-start.67 = (pred[2,128,128]{1,2,0:T(8,128)(4,1)}, pred[2,128,128]{1,2,0:T(8,128)(4,1)S(1)}, u32[]{:S(2)}) copy-start(pred[2,128,128]{1,2,0:T(8,128)(4,1)S(1)} %compare_and_fusion) | copy-start | bytes 98308
  10.6 91.6 %copy-start.35 = (f32[2,128,32]{1,2,0:T(8,128)}, f32[2,128,32]{1,2,0:T(8,128)S(1)}, u32[]{:S(2)}) copy-start(f32[2,128,32]{1,2,0:T(8,128)S(1)} %get-tuple-element.74) | copy-start | bytes 98308
  10.6 91.6 %copy-start.38 = (f32[2,128,32]{1,2,0:T(8,128)}, f32[2,128,32]{1,2,0:T(8,128)S(1)}, u32[]{:S(2)}) copy-start(f32[2,128,32]{1,2,0:T(8,128)S(1)} %get-tuple-element.75) | copy-start | bytes 98308
  10.7 21.7 %copy-start.41 = (f32[2,128,32]{1,0,2:T(2,128)}, f32[2,128,32]{1,0,2:T(2,128)S(1)}, u32[]{:S(2)}) copy-start(f32[2,128,32]{1,0,2:T(2,128)S(1)} %copy.61) | copy-start | bytes 98308
  10.8 21.7 %copy-start.45 = (f32[2,128,32]{1,0,2:T(2,128)}, f32[2,128,32]{1,0,2:T(2,128)S(1)}, u32[]{:S(2)}) copy-start(f32[2,128,32]{1,0,2:T(2,128)S(1)} %copy.62) | copy-start | bytes 98308
  20.6 13.9 %copy-start.5 = (bf16[1,576,576]{2,1,0:T(8,128)(2,1)}, bf16[1,576,576]{2,1,0:T(8,128)(2,1)S(1)}, u32[]{:S(2)}) copy-start(bf16[1,576,576]{2,1,0:T(8,128)(2,1)S(1)} %all-gather.1) | copy-start | bytes 1990660
  87.7 12.1 %copy-start.14 = (bf16[1,576,960]{2,1,0:T(8,128)(2,1)S(1)}, bf16[1,576,960]{2,1,0:T(8,128)(2,1)}, u32[]{:S(2)}) copy-start(bf16[1,576,960]{2,1,0:T(8,128)(2,1)} %all-gather.8.cloned.1.call-done) | copy-start | bytes 3317764
  87.7 11.2 %collective-permute-start = (bf16[256,576]{1,0:T(8,128)(2,1)}, bf16[256,576]{1,0:T(8,128)(2,1)S(1)}, u32[]{:S(2)}, u32[]{:S(2)}) collective-permute-start(bf16[256,576]{1,0:T(8,128)(2,1)} %fusion.44), channel_id=1, source_target_pairs={{0,16},{1,17},{2,18},{3,19},{4,20},{5,21},{6,22},{7,23},{8,24},{9,... | collective-permute-start | bytes 884744 | tf_op jit(solution)/shard_map/ppermute | solution.py:424
  100.5 1.3 copy-start.42
  100.5 1.3 copy-start.46
  101.0 1.3 copy-start.68
  102.2 2.3 copy-start.27
  102.2 2.3 copy-start.30
  102.3 2.2 copy-start.52
  102.3 2.2 copy-start.55
  104.5 2.0 copy-start.6
  104.5 2.0 copy-start.11
  104.5 2.7 copy-start
  107.1 5.0 %copy-start.1 = (f32[256,576]{1,0:T(8,128)}, f32[256,576]{1,0:T(8,128)S(1)}, u32[]{:S(2)}) copy-start(f32[256,576]{1,0:T(8,128)S(1)} %get-tuple-element.81) | copy-start | bytes 1769476
  107.2 1.5 copy-start.60
  107.2 1.7 copy-start.75
  109.0 1.6 copy-start.19
  110.6 2.4 copy-start.8
  116.0 1.8 copy-start.17
  116.0 1.8 copy-start.61
  116.0 1.9 copy-start.63
  116.0 1.9 copy-start.65
  118.3 1.4 copy-start.53
  118.3 1.4 copy-start.56
  120.2 1.2 copy-start.12
  120.2 1.4 copy-start.15
  121.6 1.1 copy-start.2
  121.6 1.2 copy-start.9
  121.6 1.4 copy-start.25
  121.6 1.4 copy-start.71
  124.1 11.2 %collective-permute-start.1 = (bf16[256,576]{1,0:T(8,128)(2,1)}, bf16[256,576]{1,0:T(8,128)(2,1)}, u32[]{:S(2)}, u32[]{:S(2)}) collective-permute-start(bf16[256,576]{1,0:T(8,128)(2,1)} %fusion.80), channel_id=1, source_target_pairs={{16,0},{17,1},{18,2},{19,3},{20,4},{21,5},{22,6},{23,7},{24,8},{25... | collective-permute-start | bytes 884744 | tf_op jit(solution)/shard_map/ppermute | solution.py:424
  136.4 8.0 %copy-start.20 = (bf16[256,576]{1,0:T(8,128)(2,1)}, bf16[256,576]{1,0:T(8,128)(2,1)S(1)}, u32[]{:S(2)}) copy-start(bf16[256,576]{1,0:T(8,128)(2,1)S(1)} %broadcast_select_fusion.refs_4_) | copy-start | bytes 884740
  140.9 1.4 copy-start.3
  144.4 1.4 copy-start.7
  144.4 1.9 copy-start.18
  144.4 1.9 copy-start.66
  147.6 1.4 copy-start.54
  147.6 1.4 copy-start.57
  147.6 1.7 copy-start.76
  148.6 1.2 copy-start.4
  148.6 1.5 copy-start.49
  150.0 1.7 copy-start.72
  150.8 2.4 copy-start.37
  150.9 2.4 copy-start.40
  154.3 1.4 copy-start.16
  155.6 1.5 copy-start.51
  155.6 1.6 copy-start.21
  155.7 1.6 copy-start.23
  286.5 4.0 %copy-start.50 = (f32[144,960]{1,0:T(8,128)S(1)}, f32[144,960]{1,0:T(8,128)}, u32[]{:S(2)}) copy-start(f32[144,960]{1,0:T(8,128)} %get-tuple-element.14) | copy-start | bytes 1658884
  286.5 4.8 %copy-start.58 = (f32[144,576]{1,0:T(8,128)S(1)}, f32[144,576]{1,0:T(8,128)}, u32[]{:S(2)}) copy-start(f32[144,576]{1,0:T(8,128)} %get-tuple-element.15) | copy-start | bytes 995332
  287.9 4.1 %copy-start.26 = (f32[144,3072]{1,0:T(8,128)S(1)}, f32[144,3072]{1,0:T(8,128)}, u32[]{:S(2)}) copy-start(f32[144,3072]{1,0:T(8,128)} %get-tuple-element.16) | copy-start | bytes 5308420
  (18 other events, 15.2 us)
Sparse Core Ops, SparseCore 0:
  9.6 20.1 all-gather.7
  31.4 30.7 all-gather.9
  63.7 20.7 all-gather.11

commit v2 on v1

--- a/solution.py
+++ b/solution.py
@@ -329,19 +329,7 @@
         def _():
             copy_c(p).start()
 
-    def stage_d(p):
-        copy_x(p).wait_recv()
-
-        @pl.when(is_middle)
-        def _():
-            totals[p][...] = (
-                send_c[p][...].astype(jnp.float32) + recv_x[p][...].astype(jnp.float32)
-            ).astype(jnp.bfloat16)
-
-        @pl.when(jnp.logical_not(is_middle))
-        def _():
-            totals[p][...] = recv_x[p][...]
-
+    def finish(p):
         @pl.when(has_outer)
         def _():
             copy_x(p).start()
@@ -353,15 +341,30 @@
             array, row, rows, column, columns = pieces[p]
             outs[array][row : row + rows, column : column + columns] = total
 
-    for step in range(count + 4):
+    def stage_middle(p):
+        copy_x(p).wait_recv()
+        totals[p][...] = (
+            send_c[p][...].astype(jnp.float32) + recv_x[p][...].astype(jnp.float32)
+        ).astype(jnp.bfloat16)
+        finish(p)
+
+    def stage_outer(p):
+        copy_x(p).wait_recv()
+        totals[p][...] = recv_x[p][...]
+        finish(p)
+
+    lag_b, lag_c, lag_d, lag_outer = 2, 5, 8, 12
+    for step in range(count + lag_outer):
         if step < count:
             stage_a(step)
-        if 0 <= step - 1 < count:
-            stage_b(step - 1)
-        if 0 <= step - 2 < count:
-            stage_c(step - 2)
-        if 0 <= step - 4 < count:
-            stage_d(step - 4)
+        if 0 <= step - lag_b < count:
+            stage_b(step - lag_b)
+        if 0 <= step - lag_c < count:
+            stage_c(step - lag_c)
+        if 0 <= step - lag_d < count:
+            pl.when(is_middle)(functools.partial(stage_middle, step - lag_d))
+        if 0 <= step - lag_outer < count:
+            pl.when(jnp.logical_not(is_middle))(functools.partial(stage_outer, step - lag_outer))
     for p in range(count):
         copy_a(p).wait_send()
         copy_b(p).wait_send()
@@ -418,6 +421,133 @@
     return results[:4], [gain_rows[i : i + 1, :width] for i in range(2)]
 
 
+def gather_kernel(halves, *refs):
+    owned, full = refs[0:4], refs[4:8]
+    near_out, near_in, far_out, far_in, side_out, pass_out, pass_in, local = refs[8:]
+    shard = lax.axis_index("shard")
+    place = lax.axis_index("replica")
+    core = shard % 2
+    row_y = shard // 2
+    sibling = row_y * 2 + (1 - core)
+    across = (1 - row_y) * 2 + core
+    parity = place % 2
+    partner = place + 1 - 2 * parity
+
+    barrier = pltpu.get_barrier_semaphore()
+    for peer in ({"shard": sibling}, {"shard": across}, {"replica": partner}):
+        pl.semaphore_signal(barrier, inc=1, device_id=peer, device_id_type=MESH_ID)
+    pl.semaphore_wait(barrier, 3)
+
+    def window(array, owner, chunk):
+        rows = owned[array].shape[0]
+        _, row, height, column, columns = chunk
+        return full[array].at[pl.ds(owner * rows + row, height), pl.ds(column, columns)]
+
+    def own(array, chunk):
+        _, row, height, column, columns = chunk
+        return owned[array].at[pl.ds(row, height), pl.ds(column, columns)]
+
+    def remote(source, target, out_sem, in_sem, device):
+        return pltpu.make_async_remote_copy(
+            src_ref=source,
+            dst_ref=target,
+            send_sem=out_sem,
+            recv_sem=in_sem,
+            device_id=device,
+            device_id_type=MESH_ID,
+        )
+
+    chunks = [(half, chunk) for half in range(2) for chunk in halves[half]]
+
+    def near(k):
+        chunk = chunks[k][1]
+        array = chunk[0]
+        return remote(
+            own(array, chunk),
+            window(array, shard, chunk),
+            near_out.at[k],
+            near_in.at[k],
+            {"shard": sibling},
+        )
+
+    def far(k):
+        chunk = chunks[k][1]
+        array = chunk[0]
+        return remote(
+            own(array, chunk),
+            window(array, shard, chunk),
+            far_out.at[k],
+            far_in.at[k],
+            {"shard": across},
+        )
+
+    def sideways(k):
+        chunk = chunks[k][1]
+        part = window(chunk[0], across, chunk)
+        return remote(part, part, side_out.at[k], far_in.at[k], {"replica": partner})
+
+    def onward(k):
+        chunk = chunks[k][1]
+        part = window(chunk[0], across, chunk)
+        return remote(part, part, pass_out.at[k], pass_in.at[k], {"shard": sibling})
+
+    def keep(array):
+        rows = owned[array].shape[0]
+        return pltpu.make_async_copy(
+            owned[array], full[array].at[pl.ds(shard * rows, rows), :], local.at[array]
+        )
+
+    indices = [[k for k, entry in enumerate(chunks) if entry[0] == half] for half in range(2)]
+
+    def flow(half):
+        mine, others = indices[half], indices[1 - half]
+        for k in mine:
+            far(k).start()
+        for k in mine + others:
+            near(k).start()
+        for array in range(4):
+            keep(array).start()
+        for j in range(max(len(mine), len(others) + 1)):
+            if j < len(mine):
+                far(mine[j]).wait_recv()
+                sideways(mine[j]).start()
+                onward(mine[j]).start()
+            if 0 <= j - 1 < len(others):
+                far(others[j - 1]).wait_recv()
+                onward(others[j - 1]).start()
+        for k in mine:
+            far(k).wait_send()
+            sideways(k).wait_send()
+        for k in mine + others:
+            near(k).wait()
+            onward(k).wait()
+        for array in range(4):
+            keep(array).wait()
+
+    for half in range(2):
+        pl.when(parity == half)(functools.partial(flow, half))
+
+
+def gather_weights(owned):
+    owners = lax.axis_size("shard")
+    cuts = split_pieces([weight.shape for weight in owned])
+    halves = [[cut for cut in cuts if cut[0] != 2], [cut for cut in cuts if cut[0] == 2]]
+    count = len(cuts)
+    anywhere = pl.BlockSpec(memory_space=pl.ANY)
+    return pl.pallas_call(
+        functools.partial(gather_kernel, halves),
+        out_shape=[
+            jax.ShapeDtypeStruct((owners * weight.shape[0], weight.shape[1]), weight.dtype)
+            for weight in owned
+        ],
+        in_specs=[anywhere] * 4,
+        out_specs=[anywhere] * 4,
+        scratch_shapes=[pltpu.SemaphoreType.DMA((count,))] * 7 + [pltpu.SemaphoreType.DMA((4,))],
+        compiler_params=pltpu.CompilerParams(collective_id=2, has_side_effects=True),
+        cost_estimate=pl.CostEstimate(flops=0, bytes_accessed=2**24, transcendentals=0),
+    )(*owned)
+
+
 def from_behind(block, axis, distance):
     devices = range(lax.axis_size(axis))
     route = [(i - distance, i) for i in devices if i - distance in devices]
@@ -437,11 +567,8 @@
 ):
     sections = lax.axis_size("section")
     section_index = lax.axis_index("section")
-    qkv_full, out_full, gate_up_full, down_full = (
-        lax.all_gather(qkv_weight[0], "shard", axis=0, tiled=True),
-        lax.all_gather(out_weight[0], "shard", axis=0, tiled=True),
-        lax.all_gather(gate_up_weight[0], "shard", axis=0, tiled=True),
-        lax.all_gather(down_weight[0], "shard", axis=0, tiled=True),
+    qkv_full, out_full, gate_up_full, down_full = gather_weights(
+        (qkv_weight[0], out_weight[0], gate_up_weight[0], down_weight[0])
     )
     weights = (attn_gain[0], qkv_full, out_full, ffn_gain[0], gate_up_full, down_full)
     geom = geometry(segments)

time: 301 us -> 249 us (0.83)
  waiting for transfers between devices: 70 us -> 11.7 us
  Pallas kernels: 124 us -> 138 us
  between operations: 15 us -> 1.7 us
  local copies, waits for them, and re-layouts: 28.7 us -> 39.1 us
  blocking collectives: 9.81 us -> 0 us
    pallas_call x0 -> x1, Pallas kernels: none -> 61.1 us  [gather_weights(): pl.pallas_call(functools.partial(gather_kernel, halves), out_shape=[jax.S...]
    all_gather x3 -> x0, waiting for transfers between devices: 54.3 us -> none  [the longest x1 26.4 us: shards(): lax.all_gather(gate_up_weight[0], 'shard', axis=0, tiled=True)]
    pallas_call x1, Pallas kernels: 124 us -> 77 us  [reduce_gradients(): pl.pallas_call(functools.partial(reduce_kernel, pieces, replicas), out_sh...]
    all_gather x1 -> x0, blocking collectives: 9.81 us -> none  [shards(): lax.all_gather(out_weight[0], 'shard', axis=0, tiled=True)]
    unnamed x167 -> x162, local copies, waits for them, and re-layouts: 18.9 us -> 22.3 us
  transfers between devices with their start and end apart: 5 -> 2, of which waited for: 5 -> 2; matrix products, arithmetic and copies ran while one was open for 5% -> 1% of each run, Pallas kernels for 0% -> 0%
where the time goes in v2:
time: 249 us; the launch traced here: 248 us
  Pallas kernels  138 us (55%)
  local copies, waits for them, and re-layouts  39.1 us (16%)
  matrix products  39 us (16%)
  other arithmetic  12.9 us (5%)
  waiting for transfers between devices  11.7 us (5%)
  starting transfers between devices  5.61 us (2%)
    pallas_call x1, Pallas kernels, reduce_gradients(): pl.pallas_call(functools.partial(reduce_kernel, pieces, replicas), out_sh...  77 us
    pallas_call x1, Pallas kernels, gather_weights(): pl.pallas_call(functools.partial(gather_kernel, halves), out_shape=[jax.S...  61.1 us
    unnamed x162, local copies, waits for them, and re-layouts  22.3 us
    ppermute x2, waiting for transfers between devices, from_behind(): return lax.ppermute(block, axis, route)  11.7 us
    dot_general x2, matrix products, layer_backward(): jnp.einsum('sd,fd->sf', out_rounded, down_layer, preferred_element_type=j...  6.03 us
    ppermute x2, starting transfers between devices, from_behind(): return lax.ppermute(block, axis, route)  5.61 us
  transfers between devices with their start and end apart: 2, of which 2 were waited for; matrix products, arithmetic and copies ran while one was open for 1% of the time, Pallas kernels for 0%

profile of v2, /device:TPU:0, one launch (start us, length us, event | category | flops | bytes accessed | tf_op | source)
XLA Modules:
  0.0 248.2 jit_solution(1996900660373962458)
XLA Ops:
  0.7 1.2 copy.72
  2.0 2.0 copy.60
  4.0 61.1 %shard_map.152 = (bf16[576,960]{1,0:T(8,128)(2,1)}, bf16[576,576]{1,0:T(8,128)(2,1)}, bf16[576,3072]{1,0:T(8,128)(2,1)}, bf16[1536,576]{1,0:T(8,128)(2,1)}) custom-call(bf16[144,960]{1,0:T(8,128)(2,1)} %bitcast.266, bf16[144,576]{1,0:T(8,128)(2,1)} %bitcast.272, bf16[144,3072]{1,0:T(8,128)(2,1)} %bitcast.256, bf16[384,576]{1,0:T(8,128)(2,1)} %bitcast.242), custom_call_target="tpu_custom_call" | custom-call | bytes 16777216 | tf_op jit(solution)/shard_map/pallas_call | solution.py:537
  65.2 2.0 fusion.59
  67.2 0.5 reshape.177
  67.7 0.7 slice.122
  70.5 1.1 fusion.125
  71.7 2.6 %fusion.21 = bf16[2,128,3,3,64]{1,4,3,2,0:T(8,128)(2,1)} fusion(f32[2,3,3,128]{3,2,1,0:T(4,128)} %fusion.125, bf16[2,128,3,64]{1,0,3,2:T(2,128)(2,1)} %slice.122, pred[2,128,128]{1,2,0:T(8,128)(4,1)} %copy-done.67, bf16[2,128,3,3,32]{1,4,3,2,0:T(8,128)(2,1)} %bitcast.276, bf16[2,128,3,3,32]{1,4,3,2,0:T(8,128)(2,1)} %bitcast.274, ...), kind=kOutput, calls=%fused_computation.55 | convolution fusion | flops 77908352 | bytes 828416 | tf_op jit(solution)/shard_map/gkrqt,gtkd->gqkrd/dot_general | solution.py:107
  74.3 1.3 copy.69
  75.5 1.8 multiply_reduce_fusion.6
  77.4 1.4 fusion.58
  78.9 1.6 fusion.18
  80.5 4.1 %collective-permute-start = (bf16[256,576]{1,0:T(8,128)(2,1)}, bf16[256,576]{1,0:T(8,128)(2,1)}, u32[]{:S(2)}, u32[]{:S(2)}) collective-permute-start(bf16[256,576]{1,0:T(8,128)(2,1)} %fusion.18), channel_id=1, source_target_pairs={{0,16},{1,17},{2,18},{3,19},{4,20},{5,21},{6,22},{7,23},{8,24},{9,... | collective-permute-start | bytes 884744 | tf_op jit(solution)/shard_map/ppermute | solution.py:554
  84.6 1.9 copy.95
  86.4 4.4 %collective-permute-done = bf16[256,576]{1,0:T(8,128)(2,1)} collective-permute-done((bf16[256,576]{1,0:T(8,128)(2,1)}, bf16[256,576]{1,0:T(8,128)(2,1)}, u32[]{:S(2)}, u32[]{:S(2)}) %collective-permute-start) | collective-permute-done | bytes 294944 | tf_op jit(solution)/shard_map/ppermute | solution.py:554
  90.8 1.2 fusion.48
  92.0 0.7 copy-done.8
  92.7 3.0 %fusion.82 = f32[256,960]{0,1:T(8,128)} fusion(bf16[576,960]{1,0:T(8,128)(2,1)} %get-tuple-element.17, bf16[256,576]{1,0:T(8,128)(2,1)S(1)} %get-tuple-element.47, f32[256]{0:T(256)S(1)} %add_rsqrt_fusion.1, f32[576]{0:T(1024)S(1)} %reduce), kind=kOutput, calls=%fused_computation.163 | convolution fusion | flops 283705344 | bytes 2387200 | tf_op jit(solution)/shard_map/dot_general | solution.py:91
  95.7 2.7 %reshape.178 = f32[2,128,15,64]{1,0,3,2:T(2,128)} reshape(f32[256,960]{0,1:T(8,128)} %fusion.82) | data formatting | bytes 1966080 | tf_op jit(solution)/shard_map/reshape | solution.py:92
  98.4 1.6 slice.129
  100.0 1.0 fusion.120
  101.0 1.4 subtract_convert_fusion.2
  102.3 0.7 copy.76
  103.0 0.7 copy.77
  103.7 0.7 subtract_convert_fusion.6
  104.4 3.2 %fusion.128 = (f32[2,3,3,128]{3,2,1,0:T(4,128)}, f32[2,3,3,128,128]{3,4,2,1,0:T(8,128)}) fusion(pred[2,128,128]{1,2,0:T(8,128)(4,1)} %copy-done.67, bf16[2,128,3,32]{1,3,2,0:T(8,128)(2,1)} %get-tuple-element.77, bf16[2,128,3,32]{1,3,2,0:T(8,128)(2,1)} %get-tuple-element.76, bf16[2,128,3,3,32]{1,4,3,2,0:T(8,128)(2,1)} %bitcast.247, ...), kind=kOutput, calls=%fused_computation.209 | convolution fusion | flops 39714944 | bytes 1614848 | tf_op jit(solution)/shard_map/sub | solution.py:104
  107.6 1.6 fusion.22
  109.6 0.6 multiply_reduce_fusion.5
  110.2 1.4 fusion.117
  112.0 1.3 multiply_convert_fusion.3
  113.6 1.5 multiply_reduce_fusion.4
  115.2 0.8 copy-done.24
  116.0 1.3 convolution_convert_fusion.3
  117.3 1.7 reshape.179
  119.0 1.8 fusion.30
  121.6 0.6 copy-done.30
  123.5 0.5 add_convert_fusion.1
  124.7 0.7 fusion.49
  126.0 1.1 fusion.39
  127.2 1.5 collective-permute-start.1
  128.7 1.7 copy.222
  130.4 7.3 %collective-permute-done.1 = bf16[256,576]{1,0:T(8,128)(2,1)} collective-permute-done((bf16[256,576]{1,0:T(8,128)(2,1)}, bf16[256,576]{1,0:T(8,128)(2,1)}, u32[]{:S(2)}, u32[]{:S(2)}) %collective-permute-start.1) | collective-permute-done | bytes 294944 | tf_op jit(solution)/shard_map/ppermute | solution.py:554
  137.7 1.0 broadcast_select_fusion.refs_4_
  138.8 4.7 %multiply_convert_fusion.1 = (bf16[256,1536]{1,0:T(8,128)(2,1)S(1)}, bf16[256,1536]{1,0:T(8,128)(2,1)S(1)}, bf16[256,1536]{1,0:T(8,128)(2,1)}) fusion(f32[256,3072]{1,0:T(8,128)} %copy-done.17, bf16[256,576]{1,0:T(8,128)(2,1)S(1)} %broadcast_select_fusion.refs_4_, bf16[1536,576]{1,0:T(8,128)(2,1)} %get-tuple-element.20), kind=kOutput, calls=%fused_computation.11 | convolution fusion | flops 458883072 | bytes 7569408 | tf_op jit(solution)/shard_map/sd,fd->sf/dot_general | solution.py:158
  143.5 2.1 multiply_reduce_fusion.2
  145.6 1.4 pad_maximum_fusion.refs_5_
  147.2 0.8 copy-done.19
  150.2 0.6 copy-done.31
  152.3 0.8 fusion.20
  153.2 0.9 copy.115
  154.1 1.2 copy.143
  156.1 0.5 add_convert_fusion
  157.9 1.5 fusion.52
  159.6 1.6 fusion.116
  161.2 0.9 copy.110
  162.0 0.9 copy.116
  162.9 0.9 copy.111
  163.8 0.6 select_maximum_fusion.refs_8_
  164.5 77.0 %shard_map.153 = (f32[384,576]{1,0:T(8,128)}, f32[144,3072]{1,0:T(8,128)}, f32[144,576]{1,0:T(8,128)}, f32[144,960]{1,0:T(8,128)}, f32[16,256]{1,0:T(8,128)}) custom-call(bf16[4,384,256]{2,1,0:T(8,128)(2,1)} %bitcast.257, bf16[4,144,256]{2,1,0:T(8,128)(2,1)} %bitcast.268, bf16[4,144,256]{2,1,0:T(8,128)(2,1)} %bitcast.267, bf16[4,144,256]{2,1,0:T(8,128)(2,1)} %bitcast.269, ...), custom_call_target="tpu_custom_call" | custom-call | flops 1811939328 | bytes 2097152 | tf_op jit(solution)/shard_map/pallas_call | solution.py:408
  241.5 1.4 fusion.124
  242.8 2.6 %copy.117 = f32[1,384,576]{1,2,0:T(8,128)} copy(f32[1,384,576]{2,1,0:T(8,128)} %bitcast.255) | data formatting | bytes 1769472
  245.4 0.8 copy.228
  246.2 0.7 copy.229
  247.0 1.2 copy.230
  (204 shorter events, 12.3 us)
Async XLA Ops:
  0.6 3.4 %copy-start.72 = (f32[1,576]{1,0:T(1,128)S(1)}, f32[1,576]{1,0:T(1,128)}, u32[]{:S(2)}) copy-start(f32[1,576]{1,0:T(1,128)} %param.12) | copy-start | bytes 6916
  1.8 65.3 %copy-start.7 = (bf16[256,576]{1,0:T(8,128)(2,1)}, bf16[256,576]{1,0:T(8,128)(2,1)S(1)}, u32[]{:S(2)}) copy-start(bf16[256,576]{1,0:T(8,128)(2,1)S(1)} %copy.72) | copy-start | bytes 884740
  67.2 1.3 copy-start.68
  67.2 1.7 copy-start.73
  69.0 0.9 copy-start.67
  71.7 5.7 %copy-start = (bf16[576,3072]{1,0:T(8,128)(2,1)S(1)}, bf16[576,3072]{1,0:T(8,128)(2,1)}, u32[]{:S(2)}) copy-start(bf16[576,3072]{1,0:T(8,128)(2,1)} %get-tuple-element.19) | copy-start | bytes 10616836
  77.3 1.5 copy-start.26
  80.5 10.4 %collective-permute-start = (bf16[256,576]{1,0:T(8,128)(2,1)}, bf16[256,576]{1,0:T(8,128)(2,1)}, u32[]{:S(2)}, u32[]{:S(2)}) collective-permute-start(bf16[256,576]{1,0:T(8,128)(2,1)} %fusion.18), channel_id=1, source_target_pairs={{0,16},{1,17},{2,18},{3,19},{4,20},{5,21},{6,22},{7,23},{8,24},{9,... | collective-permute-start | bytes 884744 | tf_op jit(solution)/shard_map/ppermute | solution.py:554
  98.4 5.4 %copy-start.37 = (f32[2,128,32]{1,2,0:T(8,128)S(1)}, f32[2,128,32]{1,2,0:T(8,128)}, u32[]{:S(2)}) copy-start(f32[2,128,32]{1,2,0:T(8,128)} %copy-done.36) | copy-start | bytes 98308
  98.4 5.4 %copy-start.41 = (f32[2,128,32]{1,2,0:T(8,128)S(1)}, f32[2,128,32]{1,2,0:T(8,128)}, u32[]{:S(2)}) copy-start(f32[2,128,32]{1,2,0:T(8,128)} %copy-done.40) | copy-start | bytes 98308
  107.6 2.0 copy-start.9
  107.6 2.0 copy-start.18
  109.6 2.1 copy-start.35
  110.2 5.0 %copy-start.1 = (f32[256,576]{1,0:T(8,128)}, f32[256,576]{1,0:T(8,128)S(1)}, u32[]{:S(2)}) copy-start(f32[256,576]{1,0:T(8,128)S(1)} %get-tuple-element.89) | copy-start | bytes 1769476
  110.2 1.8 copy-start.27
  110.2 1.8 copy-start.57
  112.0 1.6 copy-start.17
  113.6 2.3 copy-start.5
  115.1 0.8 copy-start.24
  115.2 0.8 copy-start.69
  119.0 1.8 copy-start.14
  119.0 1.8 copy-start.58
  119.0 1.9 copy-start.61
  119.0 1.9 copy-start.63
  121.3 0.9 copy-start.30
  121.3 1.0 copy-start.32
  121.3 1.4 copy-start.52
  121.3 1.4 copy-start.54
  122.3 0.8 copy-start.38
  122.3 0.8 copy-start.42
  122.7 0.8 copy-start.48
  123.3 1.2 copy-start.10
  123.3 1.4 copy-start.12
  124.7 1.1 copy-start.2
  124.7 1.2 copy-start.6
  124.7 1.4 copy-start.25
  124.7 1.4 copy-start.70
  127.2 10.6 %collective-permute-start.1 = (bf16[256,576]{1,0:T(8,128)(2,1)}, bf16[256,576]{1,0:T(8,128)(2,1)}, u32[]{:S(2)}, u32[]{:S(2)}) collective-permute-start(bf16[256,576]{1,0:T(8,128)(2,1)} %fusion.39), channel_id=1, source_target_pairs={{16,0},{17,1},{18,2},{19,3},{20,4},{21,5},{22,6},{23,7},{24,8},{25... | collective-permute-start | bytes 884744 | tf_op jit(solution)/shard_map/ppermute | solution.py:554
  138.7 8.2 %copy-start.20 = (bf16[256,576]{1,0:T(8,128)(2,1)}, bf16[256,576]{1,0:T(8,128)(2,1)S(1)}, u32[]{:S(2)}) copy-start(bf16[256,576]{1,0:T(8,128)(2,1)S(1)} %broadcast_select_fusion.refs_4_) | copy-start | bytes 884740
  138.7 4.7 %copy-start.3 = (f32[256,576]{1,0:T(8,128)S(1)}, f32[256,576]{1,0:T(8,128)}, u32[]{:S(2)}) copy-start(f32[256,576]{1,0:T(8,128)} %copy-done.1) | copy-start | bytes 1769476
  145.6 1.4 copy-start.22
  146.9 1.1 copy-start.19
  147.0 1.6 copy-start.15
  147.0 1.6 copy-start.64
  148.1 0.9 copy-start.34
  148.6 0.9 copy-start.62
  149.9 0.9 copy-start.31
  149.9 1.0 copy-start.33
  149.9 1.4 copy-start.53
  149.9 1.4 copy-start.55
  149.9 1.7 copy-start.28
  150.9 1.2 copy-start.4
  150.9 1.5 copy-start.16
  152.3 1.7 copy-start.71
  153.1 2.4 copy-start.39
  153.2 2.4 copy-start.43
  156.6 1.0 copy-start.11
  156.6 1.4 copy-start.13
  157.9 1.5 copy-start.51
  157.9 1.6 copy-start.21
  157.9 1.6 copy-start.23
  241.4 4.0 %copy-start.50 = (f32[144,960]{1,0:T(8,128)S(1)}, f32[144,960]{1,0:T(8,128)}, u32[]{:S(2)}) copy-start(f32[144,960]{1,0:T(8,128)} %get-tuple-element.22) | copy-start | bytes 1658884
  241.5 4.8 %copy-start.56 = (f32[144,576]{1,0:T(8,128)S(1)}, f32[144,576]{1,0:T(8,128)}, u32[]{:S(2)}) copy-start(f32[144,576]{1,0:T(8,128)} %get-tuple-element.23) | copy-start | bytes 995332
  242.8 4.1 %copy-start.29 = (f32[144,3072]{1,0:T(8,128)S(1)}, f32[144,3072]{1,0:T(8,128)}, u32[]{:S(2)}) copy-start(f32[144,3072]{1,0:T(8,128)} %get-tuple-element.24) | copy-start | bytes 5308420
  (12 other events, 8.1 us)

commit v3 on v2

--- a/solution.py
+++ b/solution.py
@@ -34,44 +34,139 @@
         -(jnp.arange(half_width, dtype=jnp.float32) * (2.0 / HD)) * math.log(rope_base)
     )
     angles = positions[..., None] * frequency
-    return (allowed, jnp.cos(angles), jnp.sin(angles))
-
-
-def rotate(tensor, cosine_table, sine_table):
-    half_width = tensor.shape[-1] // 2
-    first_half = tensor[..., :half_width]
-    second_half = tensor[..., half_width:]
-    cosine_table = cosine_table[..., None, :]
-    sine_table = sine_table[..., None, :]
+    cosine_half = jnp.cos(angles).reshape(-1, half_width)
+    sine_half = jnp.sin(angles).reshape(-1, half_width)
+    cosine_table = jnp.concatenate([cosine_half] * 4, axis=-1)
+    sine_table = jnp.concatenate([-sine_half, sine_half] * 2, axis=-1)
+    return (allowed.astype(jnp.int32), cosine_table, sine_table)
+
+
+GROUP = HEADS // KV
+ROTATED = (HEADS + KV) * HD
+
+
+def halves_swapped(block):
+    lane = lax.broadcasted_iota(jnp.int32, block.shape, 1)
+    ahead = pltpu.roll(block, 128 - HD // 2, 1)
+    behind = pltpu.roll(block, HD // 2, 1)
+    return jnp.where(lane % HD < HD // 2, ahead, behind)
+
+
+def head_rows(ref, start, length, kv_head):
     return jnp.concatenate(
         [
-            first_half * cosine_table - second_half * sine_table,
-            second_half * cosine_table + first_half * sine_table,
+            ref[start : start + length, head * HD : (head + 1) * HD]
+            for head in range(kv_head * GROUP, (kv_head + 1) * GROUP)
         ],
-        axis=-1,
-    )
-
-
-def unrotate(tensor, cosine_table, sine_table):
-    half_width = tensor.shape[-1] // 2
-    first_half = tensor[..., :half_width]
-    second_half = tensor[..., half_width:]
-    cosine_table = cosine_table[..., None, :]
-    sine_table = sine_table[..., None, :]
-    return jnp.concatenate(
-        [
-            first_half * cosine_table + second_half * sine_table,
-            second_half * cosine_table - first_half * sine_table,
-        ],
-        axis=-1,
-    )
-
-
-def masked_scores(query_rows, key_rows, allowed):
-    scores = jnp.einsum(
-        "gqkrd,gtkd->gkrqt", query_rows, key_rows, preferred_element_type=jnp.float32
-    ) * HD ** (-0.5)
-    return jnp.where(allowed[:, None, None], scores, masked_value)
+        axis=0,
+    )
+
+
+def matmul(left, right, left_dim, right_dim):
+    return lax.dot_general(
+        left, right, (((left_dim,), (right_dim,)), ((), ())), preferred_element_type=jnp.float32
+    )
+
+
+def attention_kernel(projected_ref, cosine_ref, sine_ref, allowed_ref, heads_ref, probs_ref, out_ref):
+    groups, length = allowed_ref.shape[:2]
+    for column in range(0, ROTATED, 128):
+        block = projected_ref[:, column : column + 128]
+        turned = block * cosine_ref[...] + halves_swapped(block) * sine_ref[...]
+        heads_ref[:, column : column + 128] = turned.astype(jnp.bfloat16)
+    heads_ref[:, ROTATED:] = projected_ref[:, ROTATED:].astype(jnp.bfloat16)
+    for group in range(groups):
+        start = group * length
+        allowed = jnp.concatenate([allowed_ref[group]] * GROUP, axis=0) > 0
+        for k in range(KV):
+            queries = head_rows(heads_ref, start, length, k)
+            keys = heads_ref[start : start + length, (HEADS + k) * HD : (HEADS + k + 1) * HD]
+            values = heads_ref[
+                start : start + length, ROTATED + k * HD : ROTATED + (k + 1) * HD
+            ]
+            scores = matmul(queries, keys, 1, 1) * HD ** (-0.5)
+            scores = jnp.where(allowed, scores, masked_value)
+            row_exp = jnp.exp(scores - jnp.max(scores, axis=-1, keepdims=True))
+            probs = row_exp / jnp.sum(row_exp, axis=-1, keepdims=True)
+            probs_ref[group, k] = probs
+            attended = matmul(probs.astype(jnp.bfloat16), values, 1, 0).astype(jnp.bfloat16)
+            for r in range(GROUP):
+                head = k * GROUP + r
+                out_ref[start : start + length, head * HD : (head + 1) * HD] = attended[
+                    r * length : (r + 1) * length
+                ]
+
+
+def attention_back_kernel(
+    heads_ref, probs_ref, grad_ref, cosine_ref, sine_ref, out_ref, turned_ref
+):
+    groups = probs_ref.shape[0]
+    length = probs_ref.shape[3]
+    for group in range(groups):
+        start = group * length
+        rows = slice(start, start + length)
+        for k in range(KV):
+            queries = head_rows(heads_ref, start, length, k)
+            grad_att = head_rows(grad_ref, start, length, k).astype(jnp.bfloat16)
+            keys = heads_ref[rows, (HEADS + k) * HD : (HEADS + k + 1) * HD]
+            values = heads_ref[rows, ROTATED + k * HD : ROTATED + (k + 1) * HD]
+            probs = probs_ref[group, k]
+            grad_values = matmul(probs.astype(jnp.bfloat16), grad_att, 0, 0)
+            grad_probs = matmul(grad_att, values, 1, 1)
+            inner = jnp.sum(probs * grad_probs, axis=-1, keepdims=True)
+            grad_scores = (probs * (grad_probs - inner)).astype(jnp.bfloat16)
+            grad_query = matmul(grad_scores, keys, 1, 0) * HD ** (-0.5)
+            grad_keys = matmul(grad_scores, queries, 0, 0) * HD ** (-0.5)
+            for r in range(GROUP):
+                head = k * GROUP + r
+                turned_ref[rows, head * HD : (head + 1) * HD] = grad_query[
+                    r * length : (r + 1) * length
+                ]
+            turned_ref[rows, (HEADS + k) * HD : (HEADS + k + 1) * HD] = grad_keys
+            out_ref[rows, ROTATED + k * HD : ROTATED + (k + 1) * HD] = grad_values.astype(
+                jnp.bfloat16
+            )
+    for column in range(0, ROTATED, 128):
+        block = turned_ref[:, column : column + 128]
+        back = block * cosine_ref[...] - halves_swapped(block) * sine_ref[...]
+        out_ref[:, column : column + 128] = back.astype(jnp.bfloat16)
+
+
+def local_call(kernel, operands, outputs, scratch=()):
+    vmem = pl.BlockSpec(memory_space=pltpu.VMEM)
+    return pl.pallas_call(
+        kernel,
+        out_shape=[jax.ShapeDtypeStruct(shape, kind) for shape, kind in outputs],
+        in_specs=[vmem] * len(operands),
+        out_specs=[vmem] * len(outputs),
+        scratch_shapes=list(scratch),
+        compiler_params=pltpu.CompilerParams(vmem_limit_bytes=32 * 2**20),
+    )(*operands)
+
+
+def attention(projected, geom):
+    allowed, cosine_table, sine_table = geom
+    groups, length = allowed.shape[:2]
+    tokens = projected.shape[0]
+    return local_call(
+        attention_kernel,
+        (projected, cosine_table, sine_table, allowed),
+        (
+            (projected.shape, jnp.bfloat16),
+            ((groups, KV, GROUP * length, length), jnp.float32),
+            ((tokens, HEADS * HD), jnp.bfloat16),
+        ),
+    )
+
+
+def attention_back(heads, probs, grad_att, geom):
+    allowed, cosine_table, sine_table = geom
+    return local_call(
+        attention_back_kernel,
+        (heads, probs, grad_att, cosine_table, sine_table),
+        ((heads.shape, jnp.bfloat16),),
+        [pltpu.VMEM((heads.shape[0], ROTATED), jnp.float32)],
+    )[0]
 
 
 def norm_back(residual, stream, inverse, gain_row, grad_out):
@@ -83,34 +178,11 @@
 
 def layer_forward(layer_in, weights, geom):
     gain_attn, qkv_layer, out_layer, gain_ffn, gate_up_layer, down_layer = weights
-    allowed, cosine_table, sine_table = geom
-    groups, length = allowed.shape[:2]
     stream = layer_in.astype(jnp.float32)
     inv_attn = lax.rsqrt(jnp.mean(stream * stream, axis=-1, keepdims=True) + norm_epsilon)
     normed = (stream * inv_attn * gain_attn).astype(jnp.bfloat16)
     projected = jnp.dot(normed, qkv_layer, preferred_element_type=jnp.float32)
-    projected = projected.reshape(groups, length, HEADS + 2 * KV, HD)
-    query_rows = projected[:, :, :HEADS]
-    key_rows = projected[:, :, HEADS : HEADS + KV]
-    value_rows = projected[:, :, HEADS + KV :].astype(jnp.bfloat16)
-    query_rows = (
-        rotate(query_rows, cosine_table, sine_table)
-        .astype(jnp.bfloat16)
-        .reshape(groups, length, KV, HEADS // KV, HD)
-    )
-    key_rows = rotate(key_rows, cosine_table, sine_table).astype(jnp.bfloat16)
-    scores = masked_scores(query_rows, key_rows, allowed)
-    row_max = jnp.max(scores, axis=-1, keepdims=True)
-    row_exp = jnp.exp(scores - row_max)
-    row_sum = jnp.sum(row_exp, axis=-1, keepdims=True)
-    attn_probs = row_exp / row_sum
-    attended = jnp.einsum(
-        "gkrqt,gtkd->gqkrd",
-        attn_probs.astype(jnp.bfloat16),
-        value_rows,
-        preferred_element_type=jnp.float32,
-    )
-    attended = attended.reshape(groups * length, HEADS * HD).astype(jnp.bfloat16)
+    heads, attn_probs, attended = attention(projected, geom)
     middle = stream + jnp.dot(attended, out_layer, preferred_element_type=jnp.float32)
     inv_ffn = lax.rsqrt(jnp.mean(middle * middle, axis=-1, keepdims=True) + norm_epsilon)
     ffn_normed = (middle * inv_ffn * gain_ffn).astype(jnp.bfloat16)
@@ -121,9 +193,7 @@
         stream,
         inv_attn,
         normed,
-        query_rows,
-        key_rows,
-        value_rows,
+        heads,
         attn_probs,
         attended,
         middle,
@@ -137,15 +207,11 @@
 
 def layer_backward(incoming, weights, geom, stored):
     gain_attn, qkv_layer, out_layer, gain_ffn, gate_up_layer, down_layer = weights
-    allowed, cosine_table, sine_table = geom
-    groups, length = allowed.shape[:2]
     (
         stream,
         inv_attn,
         normed,
-        query_rows,
-        key_rows,
-        value_rows,
+        heads,
         attn_probs,
         attended,
         middle,
@@ -168,31 +234,7 @@
     grad_middle, grad_gain_ffn = norm_back(incoming, middle, inv_ffn, gain_ffn, grad_fnorm)
     mid_rounded = grad_middle.astype(jnp.bfloat16)
     grad_att = jnp.einsum("sd,cd->sc", mid_rounded, out_layer, preferred_element_type=jnp.float32)
-    grad_att = grad_att.astype(jnp.bfloat16).reshape(groups, length, KV, HEADS // KV, HD)
-    grad_values = jnp.einsum(
-        "gkrqt,gqkrd->gtkd",
-        attn_probs.astype(jnp.bfloat16),
-        grad_att,
-        preferred_element_type=jnp.float32,
-    )
-    grad_probs = jnp.einsum(
-        "gqkrd,gtkd->gkrqt", grad_att, value_rows, preferred_element_type=jnp.float32
-    )
-    inner = jnp.sum(attn_probs * grad_probs, axis=-1, keepdims=True)
-    grad_scores = (attn_probs * (grad_probs - inner)).astype(jnp.bfloat16)
-    grad_query = jnp.einsum(
-        "gkrqt,gtkd->gqkrd", grad_scores, key_rows, preferred_element_type=jnp.float32
-    ) * HD ** (-0.5)
-    grad_keys = jnp.einsum(
-        "gkrqt,gqkrd->gtkd", grad_scores, query_rows, preferred_element_type=jnp.float32
-    ) * HD ** (-0.5)
-    grad_query = unrotate(
-        grad_query.reshape(groups, length, HEADS, HD), cosine_table, sine_table
-    ).reshape(groups * length, HEADS * HD)
-    grad_keys = unrotate(grad_keys, cosine_table, sine_table).reshape(groups * length, KV * HD)
-    grad_projected = jnp.concatenate(
-        [grad_query, grad_keys, grad_values.reshape(groups * length, KV * HD)], axis=-1
-    ).astype(jnp.bfloat16)
+    grad_projected = attention_back(heads, attn_probs, grad_att, geom)
     grad_normed = jnp.einsum(
         "se,de->sd", grad_projected, qkv_layer, preferred_element_type=jnp.float32
     )
@@ -423,20 +465,26 @@
 
 def gather_kernel(halves, *refs):
     owned, full = refs[0:4], refs[4:8]
-    near_out, near_in, far_out, far_in, side_out, pass_out, pass_in, local = refs[8:]
+    near_out, near_in, far_out, far_in, cross_out, cross_in, side_out, edge_out, local = refs[8:]
     shard = lax.axis_index("shard")
     place = lax.axis_index("replica")
     core = shard % 2
     row_y = shard // 2
     sibling = row_y * 2 + (1 - core)
     across = (1 - row_y) * 2 + core
+    diagonal = (1 - row_y) * 2 + (1 - core)
     parity = place % 2
     partner = place + 1 - 2 * parity
 
     barrier = pltpu.get_barrier_semaphore()
-    for peer in ({"shard": sibling}, {"shard": across}, {"replica": partner}):
+    for peer in (
+        {"shard": sibling},
+        {"shard": across},
+        {"shard": diagonal},
+        {"replica": partner},
+    ):
         pl.semaphore_signal(barrier, inc=1, device_id=peer, device_id_type=MESH_ID)
-    pl.semaphore_wait(barrier, 3)
+    pl.semaphore_wait(barrier, 4)
 
     def window(array, owner, chunk):
         rows = owned[array].shape[0]
@@ -486,10 +534,21 @@
         part = window(chunk[0], across, chunk)
         return remote(part, part, side_out.at[k], far_in.at[k], {"replica": partner})
 
-    def onward(k):
+    def cross(k):
         chunk = chunks[k][1]
-        part = window(chunk[0], across, chunk)
-        return remote(part, part, pass_out.at[k], pass_in.at[k], {"shard": sibling})
+        array = chunk[0]
+        return remote(
+            own(array, chunk),
+            window(array, shard, chunk),
+            cross_out.at[k],
+            cross_in.at[k],
+            {"shard": diagonal},
+        )
+
+    def edge(k):
+        chunk = chunks[k][1]
+        part = window(chunk[0], diagonal, chunk)
+        return remote(part, part, edge_out.at[k], cross_in.at[k], {"replica": partner})
 
     def keep(array):
         rows = owned[array].shape[0]
@@ -503,24 +562,26 @@
         mine, others = indices[half], indices[1 - half]
         for k in mine:
             far(k).start()
+            cross(k).start()
         for k in mine + others:
             near(k).start()
         for array in range(4):
             keep(array).start()
-        for j in range(max(len(mine), len(others) + 1)):
-            if j < len(mine):
-                far(mine[j]).wait_recv()
-                sideways(mine[j]).start()
-                onward(mine[j]).start()
-            if 0 <= j - 1 < len(others):
-                far(others[j - 1]).wait_recv()
-                onward(others[j - 1]).start()
+        for k in mine:
+            far(k).wait_recv()
+            sideways(k).start()
+            cross(k).wait_recv()
+            edge(k).start()
+        for k in others:
+            far(k).wait_recv()
+            cross(k).wait_recv()
         for k in mine:
             far(k).wait_send()
+            cross(k).wait_send()
             sideways(k).wait_send()
+            edge(k).wait_send()
         for k in mine + others:
             near(k).wait()
-            onward(k).wait()
         for array in range(4):
             keep(array).wait()
 
@@ -542,7 +603,7 @@
         ],
         in_specs=[anywhere] * 4,
         out_specs=[anywhere] * 4,
-        scratch_shapes=[pltpu.SemaphoreType.DMA((count,))] * 7 + [pltpu.SemaphoreType.DMA((4,))],
+        scratch_shapes=[pltpu.SemaphoreType.DMA((count,))] * 8 + [pltpu.SemaphoreType.DMA((4,))],
         compiler_params=pltpu.CompilerParams(collective_id=2, has_side_effects=True),
         cost_estimate=pl.CostEstimate(flops=0, bytes_accessed=2**24, transcendentals=0),
     )(*owned)

time: 249 us -> 225 us (0.904)
  local copies, waits for them, and re-layouts: 39.1 us -> 20.7 us
  matrix products: 39 us -> 21.2 us
  Pallas kernels: 138 us -> 149 us
  waiting for transfers between devices: 11.7 us -> 14.9 us
    pallas_call x0 -> x4, Pallas kernels: none -> 11.6 us  [local_call(): pl.pallas_call(kernel, out_shape=[jax.ShapeDtypeStruct(shape, kind) for s...]
    unnamed x162 -> x61, local copies, waits for them, and re-layouts: 22.3 us -> 13.2 us
    dot_general x10 -> x0, matrix products: 8.47 us -> none  [the longest x2 4.23 us: layer_forward(): jnp.einsum('gkrqt,gtkd->gqkrd', attn_probs.astype(jnp.bfloat16), value_ro...]
    reshape x8 -> x0, local copies, waits for them, and re-layouts: 5.42 us -> none  [the longest x2 3.17 us: layer_forward(): projected = projected.reshape(groups, length, HEADS + 2 * KV, HD)]
    sub x2 -> x0, matrix products: 4.38 us -> none  [layer_forward(): row_exp = jnp.exp(scores - row_max)]
    another operation x8 -> x0, other arithmetic: 3.46 us -> none
    slice x6 -> x0, local copies, waits for them, and re-layouts: 3.39 us -> none  [the longest x2 2.35 us: layer_forward(): value_rows = projected[:, :, HEADS + KV:].astype(jnp.bfloat16)]
    ppermute x2, waiting for transfers between devices: 11.7 us -> 14.9 us  [from_behind(): return lax.ppermute(block, axis, route)]
where the time goes in v3:
time: 225 us
  Pallas kernels  149 us (66%)
  matrix products  21.2 us (9%)
  local copies, waits for them, and re-layouts  20.7 us (9%)
  waiting for transfers between devices  14.9 us (7%)
  other arithmetic  12.4 us (6%)
  starting transfers between devices  5.23 us (2%)
    pallas_call x1, Pallas kernels, reduce_gradients(): pl.pallas_call(functools.partial(reduce_kernel, pieces, replicas), out_sh...  76.3 us
    pallas_call x1, Pallas kernels, gather_weights(): pl.pallas_call(functools.partial(gather_kernel, halves), out_shape=[jax.S...  61.3 us
    ppermute x2, waiting for transfers between devices, from_behind(): return lax.ppermute(block, axis, route)  14.9 us
    unnamed x61, local copies, waits for them, and re-layouts  13.2 us
    pallas_call x4, Pallas kernels, local_call(): pl.pallas_call(kernel, out_shape=[jax.ShapeDtypeStruct(shape, kind) for s...  11.6 us
    ppermute x2, starting transfers between devices, from_behind(): return lax.ppermute(block, axis, route)  5.23 us
    dot_general x2, matrix products, layer_backward(): jnp.einsum('sd,fd->sf', out_rounded, down_layer, preferred_element_type=j...  5.18 us
  transfers between devices with their start and end apart: 2, of which 2 were waited for; matrix products, arithmetic and copies ran while one was open for 1% of the time, Pallas kernels for 0%

profile of v3, /device:TPU:0, one launch (start us, length us, event | category | flops | bytes accessed | tf_op | source)
XLA Modules:
  0.0 224.7 jit_solution(14041507514329537034)
XLA Ops:
  0.7 0.7 reduce.2
  1.4 0.7 reduce
  2.1 0.9 and_convert_fusion.allowed_ref
  3.0 0.9 fusion.47
  3.9 0.1 copy.71
  4.0 0.2 reduce_window_max.15
  4.2 0.1 reduce.1
  4.3 1.2 copy.76
  5.5 0.1 fusion.25
  5.6 1.0 copy.70
  6.6 0.5 fusion.46
  7.2 0.3 pad_maximum_fusion.1
  7.5 61.3 %shard_map.152 = (bf16[576,960]{1,0:T(8,128)(2,1)}, bf16[576,576]{1,0:T(8,128)(2,1)}, bf16[576,3072]{1,0:T(8,128)(2,1)}, bf16[1536,576]{1,0:T(8,128)(2,1)}) custom-call(bf16[144,960]{1,0:T(8,128)(2,1)} %bitcast.67, bf16[144,576]{1,0:T(8,128)(2,1)} %bitcast.71, bf16[144,3072]{1,0:T(8,128)(2,1)} %bitcast.63, bf16[384,576]{1,0:T(8,128)(2,1)} %bitcast.60), custom_call_target="tpu_custom_call" | custom-call | bytes 16777216 | tf_op jit(solution)/shard_map/pallas_call | solution.py:598
  68.7 2.1 fusion.34.projected_ref
  70.8 3.3 %shard_map.153 = (bf16[256,960]{1,0:T(8,128)(2,1)}, f32[2,3,384,128]{3,2,1,0:T(8,128)}, bf16[256,576]{1,0:T(8,128)(2,1)S(1)}) custom-call(f32[256,960]{1,0:T(8,128)S(1)} %fusion.34.projected_ref, f32[256,128]{1,0:T(8,128)S(1)} %get-tuple-element.87.cosine_ref, f32[256,128]{1,0:T(8,128)S(1)} %get-tuple-element.88.sine_ref, ...), custom_call_target="tpu_custom_call" | custom-call | tf_op jit(solution)/shard_map/pallas_call | solution.py:137
  74.1 0.6 multiply_reduce_fusion.4
  74.7 1.5 fusion.33
  76.1 0.1 copy-done.16
  76.2 0.8 fusion.8
  77.1 3.7 %collective-permute-start = (bf16[256,576]{1,0:T(8,128)(2,1)S(1)}, bf16[256,576]{1,0:T(8,128)(2,1)S(1)}, u32[]{:S(2)}, u32[]{:S(2)}) collective-permute-start(bf16[256,576]{1,0:T(8,128)(2,1)S(1)} %fusion.8), channel_id=1, source_target_pairs={{0,16},{1,17},{2,18},{3,19},{4,20},{5,21},{6,22},{7,23},{8,24},{9,... | collective-permute-start | bytes 884744 | tf_op jit(solution)/shard_map/ppermute | solution.py:615
  80.8 0.9 copy.85
  81.7 6.1 %collective-permute-done = bf16[256,576]{1,0:T(8,128)(2,1)S(1)} collective-permute-done((bf16[256,576]{1,0:T(8,128)(2,1)S(1)}, bf16[256,576]{1,0:T(8,128)(2,1)S(1)}, u32[]{:S(2)}, u32[]{:S(2)}) %collective-permute-start) | collective-permute-done | bytes 294944 | tf_op jit(solution)/shard_map/ppermute | solution.py:615
  87.8 0.2 fusion.28
  88.0 0.6 fusion.44.projected_ref
  88.7 2.4 %shard_map.154 = (bf16[256,960]{1,0:T(8,128)(2,1)S(1)}, f32[2,3,384,128]{3,2,1,0:T(8,128)S(1)}, bf16[256,576]{1,0:T(8,128)(2,1)S(1)}) custom-call(f32[256,960]{1,0:T(8,128)S(1)} %fusion.44.projected_ref, f32[256,128]{1,0:T(8,128)S(1)} %get-tuple-element.87.cosine_ref, f32[256,128]{1,0:T(8,128)S(1)} %get-tuple-element.88.sine_ref, ...), custom_call_target="tpu_custom_call" | custom-call | tf_op jit(solution)/shard_map/pallas_call | solution.py:137
  91.1 0.6 multiply_reduce_fusion.3
  91.7 1.4 fusion.52
  93.1 0.1 copy-done.17
  93.2 1.3 multiply_convert_fusion.3
  94.6 0.3 copy-done.12
  94.9 1.5 multiply_reduce_fusion.2
  96.4 0.5 fusion.37.grad_ref
  97.0 3.0 %shard_map.155 = bf16[256,960]{1,0:T(8,128)(2,1)S(1)} custom-call(bf16[256,960]{1,0:T(8,128)(2,1)S(1)} %get-tuple-element.27.heads_ref, f32[2,3,384,128]{3,2,1,0:T(8,128)S(1)} %get-tuple-element.28.probs_ref, f32[256,576]{1,0:T(8,128)S(1)} %fusion.37.grad_ref, f32[256,128]{1,0:T(8,128)S(1)} %get-tuple-element.87.cosine_ref, ...), custom_call_target="tpu_custom_call" | custom-call | tf_op jit(solution)/shard_map/pallas_call | solution.py:137
  100.0 0.7 fusion.29
  100.7 1.1 fusion.19
  101.8 1.5 collective-permute-start.1
  103.3 0.9 copy.90
  104.2 8.8 %collective-permute-done.1 = bf16[256,576]{1,0:T(8,128)(2,1)} collective-permute-done((bf16[256,576]{1,0:T(8,128)(2,1)}, bf16[256,576]{1,0:T(8,128)(2,1)}, u32[]{:S(2)}, u32[]{:S(2)}) %collective-permute-start.1) | collective-permute-done | bytes 294944 | tf_op jit(solution)/shard_map/ppermute | solution.py:615
  113.0 1.0 broadcast_select_fusion.refs_4_
  114.0 3.8 %multiply_convert_fusion.1 = (bf16[256,1536]{1,0:T(8,128)(2,1)S(1)}, bf16[256,1536]{1,0:T(8,128)(2,1)S(1)}, bf16[256,1536]{1,0:T(8,128)(2,1)S(1)}) fusion(f32[256,3072]{1,0:T(8,128)} %copy-done.12, bf16[256,576]{1,0:T(8,128)(2,1)S(1)} %broadcast_select_fusion.refs_4_, bf16[1536,576]{1,0:T(8,128)(2,1)} %get-tuple-element.25), kind=kOutput, calls=%fused_computation.9 | convolution fusion | flops 458883072 | bytes 7569408 | tf_op jit(solution)/shard_map/sd,fd->sf/dot_general | solution.py:224
  117.9 2.3 %multiply_reduce_fusion = (f32[576]{0:T(1024)S(1)}, f32[256]{0:T(256)S(1)}, f32[256,576]{1,0:T(8,128)}) fusion(f32[256,576]{1,0:T(8,128)S(1)} %get-tuple-element.80, f32[256]{0:T(256)S(1)} %add_rsqrt_fusion, f32[576]{0:T(1024)S(1)} %reduce.2, bf16[576,3072]{1,0:T(8,128)(2,1)S(1)} %copy-done.3, bf16[256,1536]{1,0:T(8,128)(2,1)S(1)} %get-tuple-element.65, ...), kind=kOutput, calls=%fused_computation.53 | convolution fusion | flops 909999296 | bytes 6298112 | tf_op jit(solution)/shard_map/se,de->sd/dot_general | solution.py:233
  120.1 1.4 pad_maximum_fusion.refs_5_
  121.5 0.8 copy-done.18
  122.2 1.5 fusion.10
  123.7 1.8 copy.95
  125.6 0.1 stack_reshape.7
  125.7 2.3 %copy.111 = bf16[1536,256]{1,0:T(8,128)(2,1)} copy(bf16[1536,256]{0,1:T(8,128)(2,1)} %bitcast.59) | data formatting | bytes 1572864 | tf_op jit(solution)/shard_map/reshape | solution.py:425
  128.0 1.4 fusion.53.refs_6_
  129.4 0.7 copy-done.20
  130.1 0.5 fusion.56.grad_ref
  130.6 3.0 %shard_map.156.refs_7_ = bf16[256,960]{1,0:T(8,128)(2,1)S(1)} custom-call(bf16[256,960]{1,0:T(8,128)(2,1)S(1)} %get-tuple-element.27.heads_ref, f32[2,3,384,128]{3,2,1,0:T(8,128)S(1)} %get-tuple-element.28.probs_ref, f32[256,576]{1,0:T(8,128)S(1)} %fusion.56.grad_ref, f32[256,128]{1,0:T(8,128)S(1)} %get-tuple-element.87.cosine_ref, ...), custom_call_target="tpu_custom_call" | custom-call | tf_op jit(solution)/shard_map/pallas_call | solution.py:137
  133.6 1.5 fusion.32
  135.1 0.1 stack_reshape.6
  135.2 2.2 fusion.51
  137.4 1.8 copy.89
  139.3 0.9 copy.96
  140.2 0.9 copy.91
  141.0 0.6 select_maximum_fusion.refs_8_
  141.7 76.3 %shard_map.157 = (f32[384,576]{1,0:T(8,128)}, f32[144,3072]{1,0:T(8,128)}, f32[144,576]{1,0:T(8,128)}, f32[144,960]{1,0:T(8,128)}, f32[16,256]{1,0:T(8,128)}) custom-call(bf16[4,384,256]{2,1,0:T(8,128)(2,1)} %bitcast.64, bf16[4,144,256]{2,1,0:T(8,128)(2,1)} %bitcast.69, bf16[4,144,256]{2,1,0:T(8,128)(2,1)} %bitcast.68, bf16[4,144,256]{2,1,0:T(8,128)(2,1)} %bitcast.70, ...), custom_call_target="tpu_custom_call" | custom-call | flops 1811939328 | bytes 2097152 | tf_op jit(solution)/shard_map/pallas_call | solution.py:450
  218.0 1.4 fusion.55
  219.3 2.6 %copy.97 = f32[1,384,576]{1,2,0:T(8,128)} copy(f32[1,384,576]{2,1,0:T(8,128)} %bitcast.62) | data formatting | bytes 1769472
  221.9 0.8 copy.115
  222.7 0.7 copy.116
  223.4 1.2 copy.117
  (58 shorter events, 0.2 us)
Async XLA Ops:
  0.6 5.0 %copy-start.22 = (bf16[1,384,576]{1,2,0:T(8,128)(2,1)S(1)}, bf16[1,384,576]{1,2,0:T(8,128)(2,1)}, u32[]{:S(2)}) copy-start(bf16[1,384,576]{1,2,0:T(8,128)(2,1)} %param.17) | copy-start | bytes 1327108
  68.7 5.4 %copy-start.4 = (bf16[576,576]{1,0:T(8,128)(2,1)S(1)}, bf16[576,576]{1,0:T(8,128)(2,1)}, u32[]{:S(2)}) copy-start(bf16[576,576]{1,0:T(8,128)(2,1)} %get-tuple-element.23) | copy-start | bytes 1990660
  68.7 5.9 %copy-start.1 = (bf16[576,3072]{1,0:T(8,128)(2,1)S(1)}, bf16[576,3072]{1,0:T(8,128)(2,1)}, u32[]{:S(2)}) copy-start(bf16[576,3072]{1,0:T(8,128)(2,1)} %get-tuple-element.24) | copy-start | bytes 10616836
  74.7 1.5 copy-start.16
  76.2 4.6 %copy-start.24 = (bf16[256,576]{0,1:T(8,128)(2,1)S(1)}, bf16[256,576]{0,1:T(8,128)(2,1)}, u32[]{:S(2)}) copy-start(bf16[256,576]{0,1:T(8,128)(2,1)} %param.11) | copy-start | bytes 884740
  77.1 11.0 %copy-start.7 = (bf16[576,960]{1,0:T(8,128)(2,1)S(1)}, bf16[576,960]{1,0:T(8,128)(2,1)}, u32[]{:S(2)}) copy-start(bf16[576,960]{1,0:T(8,128)(2,1)} %get-tuple-element.21) | copy-start | bytes 3317764
  77.1 10.7 %collective-permute-start = (bf16[256,576]{1,0:T(8,128)(2,1)S(1)}, bf16[256,576]{1,0:T(8,128)(2,1)S(1)}, u32[]{:S(2)}, u32[]{:S(2)}) collective-permute-start(bf16[256,576]{1,0:T(8,128)(2,1)S(1)} %fusion.8), channel_id=1, source_target_pairs={{0,16},{1,17},{2,18},{3,19},{4,20},{5,21},{6,22},{7,23},{8,24},{9,... | collective-permute-start | bytes 884744 | tf_op jit(solution)/shard_map/ppermute | solution.py:615
  88.0 3.1 %copy-start.5 = (bf16[576,576]{1,0:T(8,128)(2,1)S(1)}, bf16[576,576]{1,0:T(8,128)(2,1)}, u32[]{:S(2)}) copy-start(bf16[576,576]{1,0:T(8,128)(2,1)} %get-tuple-element.23) | copy-start | bytes 1990660
  88.0 3.6 %copy-start.2 = (bf16[576,3072]{1,0:T(8,128)(2,1)S(1)}, bf16[576,3072]{1,0:T(8,128)(2,1)}, u32[]{:S(2)}) copy-start(bf16[576,3072]{1,0:T(8,128)(2,1)} %get-tuple-element.24) | copy-start | bytes 10616836
  91.7 1.5 copy-start.17
  91.7 1.5 copy-start.25
  93.2 1.7 copy-start.12
  94.9 1.5 copy-start.10
  97.0 3.0 %copy-start.8 = (bf16[576,960]{1,0:T(8,128)(2,1)S(1)}, bf16[576,960]{1,0:T(8,128)(2,1)}, u32[]{:S(2)}) copy-start(bf16[576,960]{1,0:T(8,128)(2,1)} %get-tuple-element.21) | copy-start | bytes 3317764
  101.8 11.2 %collective-permute-start.1 = (bf16[256,576]{1,0:T(8,128)(2,1)}, bf16[256,576]{1,0:T(8,128)(2,1)}, u32[]{:S(2)}, u32[]{:S(2)}) collective-permute-start(bf16[256,576]{1,0:T(8,128)(2,1)} %fusion.19), channel_id=1, source_target_pairs={{16,0},{17,1},{18,2},{19,3},{20,4},{21,5},{22,6},{23,7},{24,8},{25... | collective-permute-start | bytes 884744 | tf_op jit(solution)/shard_map/ppermute | solution.py:615
  114.0 14.0 %copy-start.13 = (bf16[256,576]{1,0:T(8,128)(2,1)}, bf16[256,576]{1,0:T(8,128)(2,1)S(1)}, u32[]{:S(2)}) copy-start(bf16[256,576]{1,0:T(8,128)(2,1)S(1)} %broadcast_select_fusion.refs_4_) | copy-start | bytes 884740
  114.0 3.9 %copy-start.3 = (bf16[576,3072]{1,0:T(8,128)(2,1)S(1)}, bf16[576,3072]{1,0:T(8,128)(2,1)}, u32[]{:S(2)}) copy-start(bf16[576,3072]{1,0:T(8,128)(2,1)} %get-tuple-element.24) | copy-start | bytes 10616836
  117.8 3.6 %copy-start.11 = (bf16[256,1536]{1,0:T(8,128)(2,1)}, bf16[256,1536]{1,0:T(8,128)(2,1)S(1)}, u32[]{:S(2)}) copy-start(bf16[256,1536]{1,0:T(8,128)(2,1)S(1)} %get-tuple-element.68) | copy-start | bytes 2359300
  120.1 2.1 copy-start.18
  128.0 2.2 copy-start.6
  129.4 0.7 copy-start.20
  130.6 3.0 %copy-start.9 = (bf16[576,960]{1,0:T(8,128)(2,1)S(1)}, bf16[576,960]{1,0:T(8,128)(2,1)}, u32[]{:S(2)}) copy-start(bf16[576,960]{1,0:T(8,128)(2,1)} %get-tuple-element.21) | copy-start | bytes 3317764
  133.6 3.8 %copy-start = (bf16[256,960]{1,0:T(8,128)(2,1)}, bf16[256,960]{1,0:T(8,128)(2,1)S(1)}, u32[]{:S(2)}) copy-start(bf16[256,960]{1,0:T(8,128)(2,1)S(1)} %shard_map.156.refs_7_) | copy-start | bytes 1474564
  133.6 1.6 copy-start.14
  133.6 1.6 copy-start.15
  217.9 4.0 %copy-start.21 = (f32[144,960]{1,0:T(8,128)S(1)}, f32[144,960]{1,0:T(8,128)}, u32[]{:S(2)}) copy-start(f32[144,960]{1,0:T(8,128)} %get-tuple-element.30) | copy-start | bytes 1658884
  217.9 4.8 %copy-start.23 = (f32[144,576]{1,0:T(8,128)S(1)}, f32[144,576]{1,0:T(8,128)}, u32[]{:S(2)}) copy-start(f32[144,576]{1,0:T(8,128)} %get-tuple-element.31) | copy-start | bytes 995332
  219.3 4.1 %copy-start.19 = (f32[144,3072]{1,0:T(8,128)S(1)}, f32[144,3072]{1,0:T(8,128)}, u32[]{:S(2)}) copy-start(f32[144,3072]{1,0:T(8,128)} %get-tuple-element.32) | copy-start | bytes 5308420
